TPU v7x, 512 devices: a whole 4x8x8 slice. The times are simulated.
512 devices in a mesh: lat: 32 (over x_hi, z, core), lev: 16 (over y, x_lo).
Axes of the slice: x: 4 (x_hi: 2, x_lo: 2; x = x_hi * 2 + x_lo), y: 8, z: 8, core: 2. Of those that a mesh axis runs over, the one named last changes fastest.
Arguments:
- wind_east: float32 [128, 128, 1152], P('lat', 'lev'), may hold values from -6 to 6
- wind_north: float32 [128, 128, 1152], P('lat', 'lev'), may hold values from -6 to 6
- pot_temp: float32 [128, 128, 1152], P('lat', 'lev'), may hold values from 0.5 to 2
- thickness: float32 [128, 128, 1152], P('lat', 'lev'), may hold values from 0.5 to 1.5
- source_level: int32 [128, 128, 1152], P('lat', 'lev'), may hold values from 0 to 127, as said below
- fraction: float32 [128, 128, 1152], P('lat', 'lev'), may hold values from 0 to 1
Outputs:
- east_content: float32 [128, 128, 1152], P('lat', 'lev')
- north_content: float32 [128, 128, 1152], P('lat', 'lev')
- heat_content: float32 [128, 128, 1152], P('lat', 'lev')
- new_thickness: float32 [128, 128, 1152], P('lat', 'lev')
Inputs may be any that keep to these rules, and one draw needn't show every extreme that they name: source_level at level k differs from k by at most 2; it is 0 at level 0 and 127 at the last level.
All inputs are finite; a program needn't handle non-finite values.
Results may differ from a plain program's by a relative error of at most 0.00011.
Values sent between devices are 32-bit elements; how exact they have to be, the bound alone decides.
No kernel may reach another device: no remote copies, remote signals or barrier semaphores. Data moves between devices by JAX's collectives and lax.ppermute only.
A program may use at most 64 MiB of HBM per device.

v0:
```python
import math

import jax
import jax.numpy as jnp
from jax import lax
from jax.sharding import PartitionSpec as P

STEPS = 4


def carried_in(value, axis, join, neutral):
    count, mine = (lax.axis_size(axis), lax.axis_index(axis))
    pieces = lax.all_gather(value, axis)
    pieces = pieces[::-1]
    mine = count - 1 - mine
    so_far = jnp.full_like(value, 0) + jnp.asarray(neutral, value.dtype)

    def hop(position, so_far):
        longer = join(so_far, pieces[position])
        return jnp.where(position < mine, longer, so_far)

    return lax.fori_loop(0, count - 1, hop, so_far)


def extended(block, sides, width):
    for axis, dim in sides:
        count = lax.axis_size(axis)
        forward = [(i, i + 1) for i in range(count - 1)]
        backward = [(target, source) for source, target in forward]
        low = lax.ppermute(
            lax.slice_in_dim(block, block.shape[dim] - width, None, axis=dim), axis, forward
        )
        high = lax.ppermute(lax.slice_in_dim(block, 0, width, axis=dim), axis, backward)
        block = jnp.concatenate([low, block, high], axis=dim)
    return block


def to_east(field):
    return jnp.roll(field, -1, axis=-1)


def to_west(field):
    return jnp.roll(field, 1, axis=-1)


def upwind_flux(speed, behind, ahead):
    return jnp.maximum(speed, 0.0) * behind + jnp.minimum(speed, 0.0) * ahead


def coriolis_of(row_index, lat_total):
    angle = math.pi * ((row_index.astype(jnp.float32) + 0.5) / lat_total - 0.5)
    return (0.15 * jnp.sin(angle))[:, None, None]


def load_suffix(temp_field, thick_field):
    column_load = thick_field * temp_field
    suffix_load = jnp.flip(jnp.cumsum(jnp.flip(column_load, 1), axis=1), 1)
    return (column_load, suffix_load)


def add_pair(earlier, later):
    return earlier + later


def select_near(rimmed, local_level, count):
    picked = jnp.zeros(rimmed.shape[:2] + (count,) + rimmed.shape[3:], jnp.float32)
    level_index = jnp.arange(count, dtype=jnp.int32)[None, :, None]
    for offset in range(5):
        window = rimmed[:, :, offset : offset + count]
        picked = picked + jnp.where((local_level == level_index + offset)[None], window, 0.0)
    return picked


def geopotential(temp_field, thick_field, height_scale):
    column_load, suffix_load = load_suffix(temp_field, thick_field)
    slab_total = jnp.sum(column_load, axis=1)
    load_below = carried_in(slab_total, "lev", add_pair, jnp.zeros_like(slab_total))
    return (load_below[:, None, :] + suffix_load - 0.5 * column_load) * height_scale


def advance(east_wind, north_wind, temp_field, thick_field, geopot, northern, southern, coriolis):
    wind_n, thick_n, temp_n, geo_n = northern
    wind_s, thick_s, temp_s, geo_s = southern
    new_east = east_wind - 0.05 * (to_east(geopot) - to_west(geopot)) + coriolis * north_wind
    new_north = north_wind - 0.05 * (geo_n - geo_s) - coriolis * east_wind
    flux_x = upwind_flux(0.5 * (east_wind + to_east(east_wind)), thick_field, to_east(thick_field))
    flux_up = upwind_flux(0.5 * (north_wind + wind_n), thick_field, thick_n)
    flux_down = upwind_flux(0.5 * (wind_s + north_wind), thick_s, thick_field)
    new_thick = thick_field - 0.1 * (flux_x - to_west(flux_x) + flux_up - flux_down)
    new_temp = temp_field - 0.05 * (
        east_wind * (to_east(temp_field) - to_west(temp_field)) + north_wind * (temp_n - temp_s)
    )
    return (new_east, new_north, new_temp, new_thick)


def remap_columns(column_block):
    members = column_block[:4]
    portion = column_block[4]
    source = column_block[5].astype(jnp.int32)
    level_count = members.shape[2]
    prefix = jnp.cumsum(members, axis=2) - members
    widths = ((0, 0), (0, 0), (2, 2), (0, 0))
    stacked = jnp.concatenate([jnp.pad(prefix, widths), jnp.pad(members, widths)], axis=0)
    chosen = select_near(stacked, source + 2, level_count)
    mass_at = chosen[:4] + portion[None] * chosen[4:]
    mass_prior = jnp.concatenate([jnp.zeros_like(mass_at[:, :, :1]), mass_at[:, :, :-1]], axis=2)
    return lax.all_to_all(mass_at - mass_prior, "lev", split_axis=2, concat_axis=3, tiled=True)


def body(wind_east, wind_north, pot_temp, thickness, source_level, fraction):
    lat_rows, lev_rows, lon_cells = wind_east.shape
    lat_total = lax.axis_size("lat") * lat_rows
    height_scale = 1.0 / math.sqrt(lax.axis_size("lev") * lev_rows)
    first_row = lax.axis_index("lat") * lat_rows
    east_wind, north_wind, temp_field, thick_field = (wind_east, wind_north, pot_temp, thickness)
    coriolis = coriolis_of(first_row + jnp.arange(lat_rows, dtype=jnp.int32), lat_total)
    for substep in range(STEPS):
        geopot = geopotential(temp_field, thick_field, height_scale)
        rimmed = extended(
            jnp.stack([north_wind, thick_field, temp_field, geopot]), (("lat", 1),), 1
        )
        northern = (rimmed[0, 2:], rimmed[1, 2:], rimmed[2, 2:], rimmed[3, 2:])
        southern = (rimmed[0, :-2], rimmed[1, :-2], rimmed[2, :-2], rimmed[3, :-2])
        east_wind, north_wind, temp_field, thick_field = advance(
            east_wind, north_wind, temp_field, thick_field, geopot, northern, southern, coriolis
        )
    members = jnp.stack(
        [east_wind * thick_field, north_wind * thick_field, temp_field * thick_field, thick_field]
    )
    outbound = jnp.concatenate(
        [members, jnp.stack([fraction, source_level.astype(jnp.float32)])], axis=0
    )
    contents = remap_columns(
        lax.all_to_all(outbound, "lev", split_axis=3, concat_axis=2, tiled=True)
    )
    return (contents[0], contents[1], contents[2], contents[3])


def solution(mesh):
    placed = (
        P("lat", "lev", None),
        P("lat", "lev", None),
        P("lat", "lev", None),
        P("lat", "lev", None),
        P("lat", "lev", None),
        P("lat", "lev", None),
    )
    return jax.shard_map(
        body,
        mesh=mesh,
        in_specs=placed,
        out_specs=(
            P("lat", "lev", None),
            P("lat", "lev", None),
            P("lat", "lev", None),
            P("lat", "lev", None),
        ),
        check_vma=False,
    )
```

profile of v0, /device:TPU:4, one launch (start us, length us, event | category | flops | bytes accessed | tf_op | source)
XLA Modules:
  0.0 331.3 jit_solution(8713090413330557338)
XLA Ops:
  0.6 1.0 slice.382
  2.4 1.0 slice.384
  4.1 1.1 fusion.145
  5.8 35.2 %all-gather.4 = f32[16,4,1152]{2,1,0:T(4,128)S(1)} all-gather(f32[1,4,1152]{2,1,0:T(4,128)S(1)} %copy.62), channel_id=2, replica_groups=mesh['lat'=32,'lev'=16] {'lev'}, dimensions={0}, use_global_device_ids=true | all-gather | bytes 313344 | tf_op jit(solution)/shard_map/all_gather | solution.py:13
  42.3 3.9 %collective-permute-start = (f32[4,1,8,1152]{3,2,1,0:T(8,128)S(1)}, f32[4,1,8,1152]{3,2,1,0:T(8,128)S(1)}, u32[]{:S(2)}, u32[]{:S(2)}) collective-permute-start(f32[4,1,8,1152]{3,2,1,0:T(8,128)S(1)} %get-tuple-element.450), channel_id=1, source_target_pairs={{16,0},{32,16},{48,32},{64,48},{80,64},{96,80},{112,96},{128,112},... | collective-permute-start | bytes 442376 | tf_op jit(solution)/shard_map/ppermute | solution.py:33
  46.2 1.9 collective-permute-start.1
  48.8 9.9 %collective-permute-done.1 = f32[4,1,8,1152]{3,2,1,0:T(8,128)S(1)} collective-permute-done((f32[4,1,8,1152]{3,2,1,0:T(8,128)S(1)}, f32[4,1,8,1152]{3,2,1,0:T(8,128)S(1)}, u32[]{:S(2)}, u32[]{:S(2)}) %collective-permute-start.1) | collective-permute-done | bytes 147488 | tf_op jit(solution)/shard_map/ppermute | solution.py:30
  60.2 31.1 %all-gather.5 = f32[16,4,1152]{2,1,0:T(4,128)S(1)} all-gather(f32[1,4,1152]{2,1,0:T(4,128)S(1)} %copy.64), channel_id=3, replica_groups=mesh['lat'=32,'lev'=16] {'lev'}, dimensions={0}, use_global_device_ids=true | all-gather | bytes 313344 | tf_op jit(solution)/shard_map/all_gather | solution.py:13
  92.7 1.9 collective-permute-start.2
  94.6 2.4 collective-permute-start.3
  97.3 7.7 %collective-permute-done.3 = f32[4,1,8,1152]{3,2,1,0:T(8,128)S(1)} collective-permute-done((f32[4,1,8,1152]{3,2,1,0:T(8,128)S(1)}, f32[4,1,8,1152]{3,2,1,0:T(8,128)S(1)}, u32[]{:S(2)}, u32[]{:S(2)}) %collective-permute-start.3) | collective-permute-done | bytes 147488 | tf_op jit(solution)/shard_map/ppermute | solution.py:30
  105.7 33.2 %all-gather.6 = f32[16,4,1152]{2,1,0:T(4,128)S(1)} all-gather(f32[1,4,1152]{2,1,0:T(4,128)S(1)} %copy.66), channel_id=4, replica_groups=mesh['lat'=32,'lev'=16] {'lev'}, dimensions={0}, use_global_device_ids=true | all-gather | bytes 313344 | tf_op jit(solution)/shard_map/all_gather | solution.py:13
  141.0 1.9 collective-permute-start.4
  142.9 2.4 collective-permute-start.5
  145.5 7.5 %collective-permute-done.5 = f32[4,1,8,1152]{3,2,1,0:T(8,128)S(1)} collective-permute-done((f32[4,1,8,1152]{3,2,1,0:T(8,128)S(1)}, f32[4,1,8,1152]{3,2,1,0:T(8,128)S(1)}, u32[]{:S(2)}, u32[]{:S(2)}) %collective-permute-start.5) | collective-permute-done | bytes 147488 | tf_op jit(solution)/shard_map/ppermute | solution.py:30
  154.1 31.7 %all-gather.7 = f32[16,4,1152]{2,1,0:T(4,128)S(1)} all-gather(f32[1,4,1152]{2,1,0:T(4,128)S(1)} %copy.68), channel_id=5, replica_groups=mesh['lat'=32,'lev'=16] {'lev'}, dimensions={0}, use_global_device_ids=true | all-gather | bytes 313344 | tf_op jit(solution)/shard_map/all_gather | solution.py:13
  187.5 1.9 collective-permute-start.6
  189.4 2.4 collective-permute-start.7
  192.1 7.4 %collective-permute-done.7 = f32[4,1,8,1152]{3,2,1,0:T(8,128)S(1)} collective-permute-done((f32[4,1,8,1152]{3,2,1,0:T(8,128)S(1)}, f32[4,1,8,1152]{3,2,1,0:T(8,128)S(1)}, u32[]{:S(2)}, u32[]{:S(2)}) %collective-permute-start.7) | collective-permute-done | bytes 147488 | tf_op jit(solution)/shard_map/ppermute | solution.py:30
  200.7 9.8 %copy.69 = f32[6,4,8,1152]{2,1,0,3:T(4,128)} copy(f32[6,4,8,1152]{3,2,1,0:T(8,128)S(1)} %bitcast_dynamic-update-slice_fusion) | data formatting | bytes 1769472 | tf_op jit(solution)/shard_map/concatenate | solution.py:130
  210.5 18.5 %reshape.120 = f32[16,1,13824]{2,1,0:T(1,128)} reshape(f32[1152,6,4,8]{3,2,1,0:T(4,128)} %bitcast.340) | data formatting | bytes 1769472
  228.9 5.8 %all-to-all-start = ((f32[16,1,13824]{2,1,0:T(1,128)}), f32[16,1,13824]{2,1,0:T(1,128)S(1)}, u32[]{:S(2)}, u32[]{:S(2)}) async-start(f32[16,1,13824]{2,1,0:T(1,128)} %reshape.120), calls=%async_computation | async-start | bytes 1769472 | tf_op jit(solution)/shard_map/all_to_all | solution.py:134
  234.8 19.4 %all-to-all-done = f32[16,1,13824]{2,1,0:T(1,128)S(1)} async-done(((f32[16,1,13824]{2,1,0:T(1,128)}), f32[16,1,13824]{2,1,0:T(1,128)S(1)}, u32[]{:S(2)}, u32[]{:S(2)}) %all-to-all-start) | async-done | bytes 884768 | tf_op jit(solution)/shard_map/all_to_all | solution.py:134
  254.8 2.7 reduce
  257.5 22.6 %reshape.121 = f32[1152,6,4,8]{3,2,1,0:T(4,128)} reshape(f32[16,13824]{1,0:T(8,128)S(1)} %reduce) | data formatting | bytes 1769472
  280.1 10.5 %copy.70 = f32[6,4,8,16,72]{4,2,3,1,0:T(8,128)S(1)} copy(f32[6,4,8,16,72]{2,1,0,4,3:T(4,128)} %bitcast.341) | data formatting | bytes 1769472 | tf_op jit(solution)/shard_map/all_to_all | solution.py:134
  290.8 5.5 %reduce_window_sum.44 = f32[4,4,128,72]{3,2,1,0:T(8,128)} reduce-window(f32[4,4,128,72]{3,2,1,0:T(8,128)S(1)} %slice_bitcast_fusion, f32[]{:T(128)} %constant.127.clone.1), window={size=1x1x128x1 pad=0_0x0_0x127_0x0_0}, to_apply=%region_16.17 | reduce-window | flops 18726912 | bytes 1179652 | tf_op jit(solution)/shard_map/jit(cumsum)/reduce_window_sum | solution.py:101
  296.3 1.3 fusion.132
  298.1 1.2 fusion
  300.5 26.6 %all_to_all.30 = f32[4,4,128,72]{3,1,0,2:T(4,128)S(1)} all-to-all(f32[4,4,128,72]{3,1,0,2:T(4,128)S(1)} %copy.71), channel_id=1, replica_groups=mesh['lat'=32,'lev'=16] {'lev'}, dimensions={2} | all-to-all | bytes 1179648 | tf_op jit(solution)/shard_map/all_to_all | solution.py:107
  327.6 0.8 squeeze.121
  328.6 0.8 squeeze.122
  (182 shorter events, 19.6 us)
Async XLA Ops:
  5.3 37.0 %copy-start = (f32[4,8,1152]{2,1,0:T(8,128)S(1)}, f32[4,8,1152]{2,1,0:T(8,128)}, u32[]{:S(2)}) copy-start(f32[4,8,1152]{2,1,0:T(8,128)} %param.16) | copy-start | bytes 442372
  5.3 37.0 %copy-start.1 = (f32[4,8,1152]{2,1,0:T(8,128)S(1)}, f32[4,8,1152]{2,1,0:T(8,128)}, u32[]{:S(2)}) copy-start(f32[4,8,1152]{2,1,0:T(8,128)} %param.17) | copy-start | bytes 442372
  5.3 37.0 %copy-start.2 = (f32[4,8,1152]{2,1,0:T(8,128)S(1)}, f32[4,8,1152]{2,1,0:T(8,128)}, u32[]{:S(2)}) copy-start(f32[4,8,1152]{2,1,0:T(8,128)} %param.15) | copy-start | bytes 442372
  41.0 17.8 %copy-start.3 = (f32[4,8,1152]{2,1,0:T(8,128)S(1)}, f32[4,8,1152]{2,1,0:T(8,128)}, u32[]{:S(2)}) copy-start(f32[4,8,1152]{2,1,0:T(8,128)} %param.14) | copy-start | bytes 442372
  42.3 6.6 %collective-permute-start = (f32[4,1,8,1152]{3,2,1,0:T(8,128)S(1)}, f32[4,1,8,1152]{3,2,1,0:T(8,128)S(1)}, u32[]{:S(2)}, u32[]{:S(2)}) collective-permute-start(f32[4,1,8,1152]{3,2,1,0:T(8,128)S(1)} %get-tuple-element.450), channel_id=1, source_target_pairs={{16,0},{32,16},{48,32},{64,48},{80,64},{96,80},{112,96},{128,112},... | collective-permute-start | bytes 442376 | tf_op jit(solution)/shard_map/ppermute | solution.py:33
  46.2 12.6 %collective-permute-start.1 = (f32[4,1,8,1152]{3,2,1,0:T(8,128)S(1)}, f32[4,1,8,1152]{3,2,1,0:T(8,128)S(1)}, u32[]{:S(2)}, u32[]{:S(2)}) collective-permute-start(f32[4,1,8,1152]{3,2,1,0:T(8,128)S(1)} %get-tuple-element.451), channel_id=1, source_target_pairs={{0,16},{16,32},{32,48},{48,64},{64,80},{80,96},{96,112},{112,128},... | collective-permute-start | bytes 442376 | tf_op jit(solution)/shard_map/ppermute | solution.py:30
  92.7 4.6 %collective-permute-start.2 = (f32[4,1,8,1152]{3,2,1,0:T(8,128)S(1)}, f32[4,1,8,1152]{3,2,1,0:T(8,128)S(1)}, u32[]{:S(2)}, u32[]{:S(2)}) collective-permute-start(f32[4,1,8,1152]{3,2,1,0:T(8,128)S(1)} %get-tuple-element.448), channel_id=1, source_target_pairs={{16,0},{32,16},{48,32},{64,48},{80,64},{96,80},{112,96},{128,112},... | collective-permute-start | bytes 442376 | tf_op jit(solution)/shard_map/ppermute | solution.py:33
  94.6 10.4 %collective-permute-start.3 = (f32[4,1,8,1152]{3,2,1,0:T(8,128)S(1)}, f32[4,1,8,1152]{3,2,1,0:T(8,128)S(1)}, u32[]{:S(2)}, u32[]{:S(2)}) collective-permute-start(f32[4,1,8,1152]{3,2,1,0:T(8,128)S(1)} %get-tuple-element.449), channel_id=1, source_target_pairs={{0,16},{16,32},{32,48},{48,64},{64,80},{80,96},{96,112},{112,128},... | collective-permute-start | bytes 442376 | tf_op jit(solution)/shard_map/ppermute | solution.py:30
  141.0 4.6 %collective-permute-start.4 = (f32[4,1,8,1152]{3,2,1,0:T(8,128)S(1)}, f32[4,1,8,1152]{3,2,1,0:T(8,128)S(1)}, u32[]{:S(2)}, u32[]{:S(2)}) collective-permute-start(f32[4,1,8,1152]{3,2,1,0:T(8,128)S(1)} %get-tuple-element.446), channel_id=1, source_target_pairs={{16,0},{32,16},{48,32},{64,48},{80,64},{96,80},{112,96},{128,112},... | collective-permute-start | bytes 442376 | tf_op jit(solution)/shard_map/ppermute | solution.py:33
  142.9 10.2 %collective-permute-start.5 = (f32[4,1,8,1152]{3,2,1,0:T(8,128)S(1)}, f32[4,1,8,1152]{3,2,1,0:T(8,128)S(1)}, u32[]{:S(2)}, u32[]{:S(2)}) collective-permute-start(f32[4,1,8,1152]{3,2,1,0:T(8,128)S(1)} %get-tuple-element.447), channel_id=1, source_target_pairs={{0,16},{16,32},{32,48},{48,64},{64,80},{80,96},{96,112},{112,128},... | collective-permute-start | bytes 442376 | tf_op jit(solution)/shard_map/ppermute | solution.py:30
  187.5 4.6 %collective-permute-start.6 = (f32[4,1,8,1152]{3,2,1,0:T(8,128)S(1)}, f32[4,1,8,1152]{3,2,1,0:T(8,128)S(1)}, u32[]{:S(2)}, u32[]{:S(2)}) collective-permute-start(f32[4,1,8,1152]{3,2,1,0:T(8,128)S(1)} %get-tuple-element.444), channel_id=1, source_target_pairs={{16,0},{32,16},{48,32},{64,48},{80,64},{96,80},{112,96},{128,112},... | collective-permute-start | bytes 442376 | tf_op jit(solution)/shard_map/ppermute | solution.py:33
  189.4 10.1 %collective-permute-start.7 = (f32[4,1,8,1152]{3,2,1,0:T(8,128)S(1)}, f32[4,1,8,1152]{3,2,1,0:T(8,128)S(1)}, u32[]{:S(2)}, u32[]{:S(2)}) collective-permute-start(f32[4,1,8,1152]{3,2,1,0:T(8,128)S(1)} %get-tuple-element.445), channel_id=1, source_target_pairs={{0,16},{16,32},{32,48},{48,64},{64,80},{80,96},{96,112},{112,128},... | collective-permute-start | bytes 442376 | tf_op jit(solution)/shard_map/ppermute | solution.py:30
  199.7 0.9 copy-start.4
  199.7 1.0 copy-start.5
  228.9 25.3 %all-to-all-start = ((f32[16,1,13824]{2,1,0:T(1,128)}), f32[16,1,13824]{2,1,0:T(1,128)S(1)}, u32[]{:S(2)}, u32[]{:S(2)}) async-start(f32[16,1,13824]{2,1,0:T(1,128)} %reshape.120), calls=%async_computation | async-start | bytes 1769472 | tf_op jit(solution)/shard_map/all_to_all | solution.py:134
where the time goes:
time: 332 us; the launch traced here: 331 us
  blocking collectives  158 us (48%)
  local copies, waits for them, and re-layouts  76.6 us (23%)
  waiting for transfers between devices  52.8 us (16%)
  starting transfers between devices  24.6 us (7%)
  other arithmetic  16.6 us (5%)
    all_gather x4, blocking collectives, carried_in(): pieces = lax.all_gather(value, axis)  131 us
    unnamed x24, local copies, waits for them, and re-layouts  43.6 us
    ppermute x4, waiting for transfers between devices, extended(): lax.ppermute(lax.slice_in_dim(block, block.shape[dim] - width, None, axis...  32.6 us
    all_to_all x1, blocking collectives, remap_columns(): lax.all_to_all(mass_at - mass_prior, 'lev', split_axis=2, concat_axis=3,...  26.6 us
    all_to_all x1, waiting for transfers between devices, body(): lax.all_to_all(outbound, 'lev', split_axis=3, concat_axis=2, tiled=True)  19.4 us
    all_to_all x2, local copies, waits for them, and re-layouts, body(): lax.all_to_all(outbound, 'lev', split_axis=3, concat_axis=2, tiled=True)  11 us
    concatenate x1, local copies, waits for them, and re-layouts, body(): jnp.concatenate([members, jnp.stack([fraction, source_level.astype(jnp.fl...  9.77 us
    ppermute x4, starting transfers between devices, extended(): lax.ppermute(lax.slice_in_dim(block, 0, width, axis=dim), axis, backward)  9.66 us
  transfers between devices with their start and end apart: 9, of which 9 were waited for; matrix products, arithmetic and copies ran while one was open for 0% of the time, Pallas kernels for 0%

commit v1 on v0

v1 whole, which is shorter than its diff:
```python
import functools
import math

import jax
import jax.numpy as jnp
from jax import lax
from jax.experimental import pallas as pl
from jax.experimental.pallas import tpu as pltpu
from jax.sharding import PartitionSpec as P

STEPS = 4
LANES = 128
BLOCK = 8


def send_kernel(u_ref, v_ref, t_ref, d_ref, f_ref, s_ref, state_ref, target_ref, wide, narrow):
    lon = u_ref.shape[-1]
    count, width, _ = state_ref.shape
    chunk = lon // count
    half = chunk // 2
    rim = (width - chunk) // 2
    levels = s_ref[...].astype(jnp.float32)
    for at in range(0, lon, LANES):
        cols = slice(at, at + LANES)
        block = jnp.concatenate(
            [ref[:, :, cols].reshape(-1, LANES) for ref in (u_ref, v_ref, t_ref, d_ref)], axis=0
        )
        wide[BLOCK + at : BLOCK + at + LANES, :] = block.T
        pair = [f_ref[:, :, cols].reshape(-1, LANES), levels[:, :, cols].reshape(-1, LANES)]
        narrow[at : at + LANES, :] = jnp.concatenate(pair + pair, axis=0).T
    wide[:BLOCK, :] = wide[lon : lon + BLOCK, :]
    wide[lon + BLOCK :, :] = wide[BLOCK : 2 * BLOCK, :]
    narrow[lon:, :] = jnp.zeros((narrow.shape[0] - lon, LANES), jnp.float32)
    rows = target_ref.shape[1]
    first = lax.broadcasted_iota(jnp.int32, (rows, LANES), 1) < LANES // 2
    for c in range(count):
        at = BLOCK + c * chunk - rim
        state_ref[c] = wide[at : at + width, :]
        at = c * chunk
        target_ref[c] = jnp.where(
            first, narrow[at : at + rows, :], narrow[at + half : at + half + rows, :]
        )


def swap_blocks(tiles):
    lane = lax.broadcasted_iota(jnp.int32, tiles[0].shape, 1) // BLOCK
    count = len(tiles)
    tiles = list(tiles)
    bit = 1
    while bit < count:
        upper = (lane & bit) != 0
        for low in range(count):
            if low & bit:
                continue
            high = low | bit
            a, b = tiles[low], tiles[high]
            tiles[low] = jnp.where(upper, pltpu.roll(b, bit * BLOCK, 1), a)
            tiles[high] = jnp.where(upper, b, pltpu.roll(a, LANES - bit * BLOCK, 1))
        bit *= 2
    return tiles


def split3(x):
    hi = x.astype(jnp.bfloat16)
    rest = x - hi.astype(jnp.float32)
    mid = rest.astype(jnp.bfloat16)
    low = (rest - mid.astype(jnp.float32)).astype(jnp.bfloat16)
    return hi, mid, low


def times_exact(x, matrix):
    return sum(jnp.dot(part, matrix, preferred_element_type=jnp.float32) for part in split3(x))


def core_kernel(own_ref, north_ref, south_ref, target_ref, out_ref, *scratch):
    state = (scratch[0:4], scratch[4:8])
    geo, place, result = scratch[8:11]
    count, width, _ = own_ref.shape
    chunk = out_ref.shape[1]
    half = chunk // 2
    rim = (width - chunk) // 2
    lat = lax.axis_index("lat")
    lat_total = lax.axis_size("lat") * 4
    rows = 12

    def unpack(i, carry):
        at = pl.ds(pl.multiple_of(i * BLOCK, BLOCK), BLOCK)
        for ref, base in ((south_ref, 0), (own_ref, 4), (north_ref, 8)):
            tiles = swap_blocks([ref[s, at, :] for s in range(count)])
            for f in range(4):
                for r in range(4):
                    state[0][f][base + r, at, :] = tiles[4 * f + r]
        return carry

    lax.fori_loop(0, width // BLOCK, unpack, 0)

    for i in range(target_ref.shape[1] // BLOCK):
        at = pl.ds(i * BLOCK, BLOCK)
        tiles = swap_blocks([target_ref[s, at, :] for s in range(count)])
        for j in range(2):
            keep = min(BLOCK, half - i * BLOCK)
            for k in range(8):
                place[k, j * half + i * BLOCK : j * half + i * BLOCK + keep, :] = tiles[8 * j + k][:keep]

    row_level = lax.broadcasted_iota(jnp.int32, (LANES, LANES), 0)
    col_level = lax.broadcasted_iota(jnp.int32, (LANES, LANES), 1)
    below = jnp.where(row_level > col_level, 1.0, jnp.where(row_level == col_level, 0.5, 0.0))
    below = below.astype(jnp.bfloat16)
    above = jnp.where(row_level < col_level, 1.0, 0.0).astype(jnp.bfloat16)
    slope = 0.05 / math.sqrt(LANES)

    row_index = lax.broadcasted_iota(jnp.int32, (16, LANES), 0) + (lat * 4 - 4)
    angle = math.pi * ((row_index.astype(jnp.float32) + 0.5) / lat_total - 0.5)
    result[0, :16, :] = 0.15 * jnp.sin(angle)

    def east(x):
        return pltpu.roll(x, width - 1, 0)

    def west(x):
        return pltpu.roll(x, 1, 0)

    def upwind(speed, behind, ahead):
        return jnp.maximum(speed, 0.0) * behind + jnp.minimum(speed, 0.0) * ahead

    for step in range(STEPS):
        u_ref, v_ref, t_ref, d_ref = state[step % 2]
        new = state[1 - step % 2]

        def potential(j, carry):
            geo[j] = times_exact(d_ref[j] * t_ref[j], below)
            return carry

        lax.fori_loop(step, rows - step, potential, 0)

        def advance(j, flux_down):
            u, v, t, d = u_ref[j], v_ref[j], t_ref[j], d_ref[j]
            v_n, d_n = v_ref[j + 1], d_ref[j + 1]
            g = geo[j]
            cor = result[0, pl.ds(j, 1), :]
            inside = jnp.logical_and(lat * 4 - 4 + j >= 0, lat * 4 - 4 + j < lat_total)
            d_e = east(d)
            flux_x = upwind(0.5 * (u + east(u)), d, d_e)
            flux_up = upwind(0.5 * (v + v_n), d, d_n)
            new_u = u - slope * (east(g) - west(g)) + cor * v
            new_v = v - slope * (geo[j + 1] - geo[j - 1]) - cor * u
            new_d = d - 0.1 * (flux_x - west(flux_x) + flux_up - flux_down)
            new_t = t - 0.05 * (u * (east(t) - west(t)) + v * (t_ref[j + 1] - t_ref[j - 1]))
            for ref, value in zip(new, (new_u, new_v, new_t, new_d)):
                ref[j] = jnp.where(inside, value, 0.0)
            return flux_up

        first = step + 1
        flux_start = upwind(0.5 * (v_ref[step] + v_ref[first]), d_ref[step], d_ref[first])
        lax.fori_loop(first, rows - first, advance, flux_start)

    final = state[STEPS % 2]
    lane = lax.broadcasted_iota(jnp.int32, (chunk, LANES), 1)

    def remap(r, carry):
        source = place[4 + r].astype(jnp.int32)
        part = place[r]
        mid = pl.ds(rim, chunk)
        u, v, t, d = (ref[4 + r, mid, :] for ref in final)
        for f, q in enumerate((u * d, v * d, t * d, d)):
            prefix = times_exact(q, above)
            mass = jnp.take_along_axis(prefix, source, axis=1) + part * jnp.take_along_axis(
                q, source, axis=1
            )
            result[4 * f + r] = mass - jnp.where(lane == 0, 0.0, pltpu.roll(mass, 1, 1))
        return carry

    lax.fori_loop(0, 4, remap, 0)

    def pack(i, carry):
        at = pl.ds(pl.multiple_of(i * BLOCK, BLOCK), BLOCK)
        for s, tile in enumerate(swap_blocks([result[k, at, :] for k in range(count)])):
            out_ref[s, at, :] = tile
        return carry

    lax.fori_loop(0, chunk // BLOCK, pack, 0)


def receive_kernel(in_ref, *out_refs):
    lon = out_refs[0].shape[-1]
    flat = in_ref[...].reshape(lon, LANES)
    for at in range(0, lon, LANES):
        block = flat[at : at + LANES, :].T
        for f, ref in enumerate(out_refs):
            ref[:, :, at : at + LANES] = block[32 * f : 32 * f + 32].reshape(4, 8, LANES)


def whole(count):
    return [pl.BlockSpec(memory_space=pltpu.VMEM)] * count


def call(kernel, shapes, scratch, *args):
    out_shape = [jax.ShapeDtypeStruct(shape, jnp.float32) for shape in shapes]
    return pl.pallas_call(
        kernel,
        out_shape=out_shape,
        in_specs=whole(len(args)),
        out_specs=whole(len(out_shape)),
        scratch_shapes=[pltpu.VMEM(shape, jnp.float32) for shape in scratch],
        compiler_params=pltpu.CompilerParams(vmem_limit_bytes=40 * 2**20),
    )(*args)


def body(wind_east, wind_north, pot_temp, thickness, source_level, fraction):
    lon = wind_east.shape[-1]
    count = lax.axis_size("lev")
    blocks = lax.axis_size("lat")
    chunk = lon // count
    width = chunk + 2 * STEPS
    narrow = -(-(chunk // 2) // BLOCK) * BLOCK
    state, target = call(
        send_kernel,
        [(count, width, LANES), (count, narrow, LANES)],
        [(lon + 2 * BLOCK, LANES), (lon + BLOCK, LANES)],
        wind_east, wind_north, pot_temp, thickness, fraction, source_level,
    )
    own = lax.all_to_all(state, "lev", 0, 0, tiled=True)
    north = lax.ppermute(own, "lat", [(i + 1, i) for i in range(blocks - 1)])
    south = lax.ppermute(own, "lat", [(i, i + 1) for i in range(blocks - 1)])
    own, target = lax.optimization_barrier((own, target))
    target = lax.all_to_all(target, "lev", 0, 0, tiled=True)
    field = (12, width, LANES)
    (contents,) = call(
        core_kernel,
        [(count, chunk, LANES)],
        [field] * 9 + [(8, chunk, LANES), (16, chunk, LANES)],
        own, north, south, target,
    )
    contents = lax.all_to_all(contents, "lev", 0, 0, tiled=True)
    return tuple(call(receive_kernel, [wind_east.shape] * 4, [], contents))


def solution(mesh):
    placed = P("lat", "lev", None)
    return jax.shard_map(
        body, mesh=mesh, in_specs=(placed,) * 6, out_specs=(placed,) * 4, check_vma=False
    )
```

time: 332 us -> 100 us (0.30)
  the two profiles are of different devices: /device:TPU:4 before, /device:TPU:192 now
where the time goes in v1:
time: 100 us; the launch traced here: 99.7 us
  blocking collectives  69.1 us (69%)
  Pallas kernels  18.9 us (19%)
  starting transfers between devices  5.55 us (6%)
  local copies, waits for them, and re-layouts  5.45 us (5%)
    all_to_all x1, blocking collectives, body(): own = lax.all_to_all(state, 'lev', 0, 0, tiled=True)  28.8 us
    all_to_all x1, blocking collectives, body(): contents = lax.all_to_all(contents, 'lev', 0, 0, tiled=True)  24.2 us
    pallas_call x3, Pallas kernels, call(): pl.pallas_call(kernel, out_shape=out_shape, in_specs=whole(len(args)), ou...  18.9 us
    all_to_all x1, blocking collectives, body(): target = lax.all_to_all(target, 'lev', 0, 0, tiled=True)  16.1 us
    unnamed x12, local copies, waits for them, and re-layouts  5.45 us
    ppermute x1, starting transfers between devices, body(): north = lax.ppermute(own, 'lat', [(i + 1, i) for i in range(blocks - 1)])  3.64 us
  transfers between devices with their start and end apart: 2, of which 0 were waited for; matrix products, arithmetic and copies ran while one was open for 0% of the time, Pallas kernels for 0%

profile of v1, /device:TPU:192, one launch (start us, length us, event | category | flops | bytes accessed | tf_op | source)
XLA Modules:
  0.0 99.7 jit_solution(16805623954515479444)
XLA Ops:
  0.6 0.0 copy-start
  0.6 0.9 copy-done
  1.5 0.0 copy-start.1
  1.5 0.9 copy-done.1
  2.5 0.0 copy-start.2
  2.5 0.9 copy-done.2
  3.4 0.0 copy-start.3
  3.4 0.9 copy-done.3
  4.3 0.0 copy-start.4
  4.3 0.9 copy-done.4
  5.2 0.0 copy-start.5
  5.2 0.9 copy-done.5
  6.1 0.5 shard_map.93
  6.6 28.8 %all_to_all.15.own_ref = f32[16,80,128]{2,1,0:T(8,128)S(1)} all-to-all(f32[16,80,128]{2,1,0:T(8,128)S(1)} %get-tuple-element.8), channel_id=1, replica_groups=mesh['lat'=32,'lev'=16] {'lev'}, dimensions={0} | all-to-all | bytes 1310720 | tf_op jit(solution)/shard_map/all_to_all | solution.py:221
  35.4 1.9 %collective-permute-start.1 = (f32[16,80,128]{2,1,0:T(8,128)S(1)}, f32[16,80,128]{2,1,0:T(8,128)S(1)}, u32[]{:S(2)}, u32[]{:S(2)}) collective-permute-start(f32[16,80,128]{2,1,0:T(8,128)S(1)} %all_to_all.15.own_ref), channel_id=1, source_target_pairs={{0,16},{16,32},{32,48},{48,64},{64,80},{80,96},{96,112},{112,128},... | collective-permute-start | bytes 1966088 | tf_op jit(solution)/shard_map/ppermute | solution.py:223
  37.3 3.6 %collective-permute-start = (f32[16,80,128]{2,1,0:T(8,128)S(1)}, f32[16,80,128]{2,1,0:T(8,128)S(1)}, u32[]{:S(2)}, u32[]{:S(2)}) collective-permute-start(f32[16,80,128]{2,1,0:T(8,128)S(1)} %all_to_all.15.own_ref), channel_id=1, source_target_pairs={{16,0},{32,16},{48,32},{64,48},{80,64},{96,80},{112,96},{128,112},... | collective-permute-start | bytes 1966088 | tf_op jit(solution)/shard_map/ppermute | solution.py:222
  40.9 16.1 %all_to_all.16.target_ref = f32[16,40,128]{2,1,0:T(8,128)S(1)} all-to-all(f32[16,40,128]{2,1,0:T(8,128)S(1)} %get-tuple-element.11), channel_id=1, replica_groups=mesh['lat'=32,'lev'=16] {'lev'}, dimensions={0} | all-to-all | bytes 655360 | tf_op jit(solution)/shard_map/all_to_all | solution.py:225
  57.1 0.0 collective-permute-done.1.south_ref
  57.1 0.0 collective-permute-done.north_ref
  57.1 17.4 %shard_map.94 = f32[16,72,128]{2,1,0:T(8,128)S(1)} custom-call(f32[16,80,128]{2,1,0:T(8,128)S(1)} %all_to_all.15.own_ref, f32[16,80,128]{2,1,0:T(8,128)S(1)} %collective-permute-done.north_ref, f32[16,80,128]{2,1,0:T(8,128)S(1)} %collective-permute-done.1.south_ref, f32[16,40,128]{2,1,0:T(8,128)S(1)} %all_to_all.16.target_ref), custom_call_target="tpu_custom_call" | custom-call | tf_op jit(solution)/shard_map/pallas_call | solution.py:198
  74.5 24.2 %all_to_all.17.in_ref = f32[16,72,128]{2,1,0:T(8,128)S(1)} all-to-all(f32[16,72,128]{2,1,0:T(8,128)S(1)} %shard_map.94), channel_id=1, replica_groups=mesh['lat'=32,'lev'=16] {'lev'}, dimensions={0} | all-to-all | bytes 1179648 | tf_op jit(solution)/shard_map/all_to_all | solution.py:233
  98.7 1.0 %shard_map.95 = (f32[4,8,1152]{2,1,0:T(8,128)}, f32[4,8,1152]{2,1,0:T(8,128)}, f32[4,8,1152]{2,1,0:T(8,128)}, f32[4,8,1152]{2,1,0:T(8,128)}) custom-call(f32[16,72,128]{2,1,0:T(8,128)S(1)} %all_to_all.17.in_ref), custom_call_target="tpu_custom_call" | custom-call | tf_op jit(solution)/shard_map/pallas_call | solution.py:198
Async XLA Ops:
  0.6 0.9 copy-start
  1.5 0.9 copy-start.1
  2.5 0.9 copy-start.2
  3.4 0.9 copy-start.3
  4.3 0.9 copy-start.4
  5.2 0.9 copy-start.5
  35.4 21.7 %collective-permute-start.1 = (f32[16,80,128]{2,1,0:T(8,128)S(1)}, f32[16,80,128]{2,1,0:T(8,128)S(1)}, u32[]{:S(2)}, u32[]{:S(2)}) collective-permute-start(f32[16,80,128]{2,1,0:T(8,128)S(1)} %all_to_all.15.own_ref), channel_id=1, source_target_pairs={{0,16},{16,32},{32,48},{48,64},{64,80},{80,96},{96,112},{112,128},... | collective-permute-start | bytes 1966088 | tf_op jit(solution)/shard_map/ppermute | solution.py:223
  37.3 19.8 %collective-permute-start = (f32[16,80,128]{2,1,0:T(8,128)S(1)}, f32[16,80,128]{2,1,0:T(8,128)S(1)}, u32[]{:S(2)}, u32[]{:S(2)}) collective-permute-start(f32[16,80,128]{2,1,0:T(8,128)S(1)} %all_to_all.15.own_ref), channel_id=1, source_target_pairs={{16,0},{32,16},{48,32},{64,48},{80,64},{96,80},{112,96},{128,112},... | collective-permute-start | bytes 1966088 | tf_op jit(solution)/shard_map/ppermute | solution.py:222

commit v2 on v1

v2 whole, which is shorter than its diff:
```python
import math

import jax
import jax.numpy as jnp
from jax import lax
from jax.experimental import pallas as pl
from jax.experimental.pallas import tpu as pltpu
from jax.sharding import PartitionSpec as P

STEPS = 4
LANES = 128
BLOCK = 8


def send_kernel(u_in, v_in, t_in, d_in, f_in, s_in, state_out, target_out, *scratch):
    fields, levels = scratch[:5], scratch[5]
    wide_stack, narrow_stack, wide, narrow, state_ref, target_ref, sems = scratch[6:]
    rows, _, lon = u_in.shape
    count, width, _ = state_ref.shape
    chunk = lon // count
    half = chunk // 2
    rim = (width - chunk) // 2
    mine = lax.axis_index("lev")
    copies = [
        pltpu.make_async_copy(source, target, sems.at[i])
        for i, (source, target) in enumerate(
            zip((u_in, v_in, t_in, d_in, f_in, s_in), fields + (levels,))
        )
    ]
    for copy in copies:
        copy.start()

    def block(j):
        return lax.rem(mine + j, count)

    for f in range(4):
        copies[f].wait()
        for r in range(rows):
            wide_stack[block(rows * f + r)] = fields[f][r]
    for at in range(0, lon, LANES):
        wide[BLOCK + at : BLOCK + at + LANES, :] = (
            wide_stack[:, :, at : at + LANES].reshape(LANES, LANES).T
        )
    wide[:BLOCK, :] = wide[lon : lon + BLOCK, :]
    wide[lon + BLOCK :, :] = wide[BLOCK : 2 * BLOCK, :]
    for c in range(count):
        at = BLOCK + c * chunk - rim
        state_ref[c] = wide[at : at + width, :]
    out = [pltpu.make_async_copy(state_ref, state_out, sems.at[0])]
    out[0].start()

    copies[4].wait()
    copies[5].wait()
    for h in range(2):
        for r in range(rows):
            narrow_stack[block(8 * h + r)] = fields[4][r]
            narrow_stack[block(8 * h + 4 + r)] = levels[r].astype(jnp.float32)
    for at in range(0, lon, LANES):
        narrow[at : at + LANES, :] = narrow_stack[:, :, at : at + LANES].reshape(LANES, LANES).T
    narrow[lon:, :] = jnp.zeros((narrow.shape[0] - lon, LANES), jnp.float32)
    size = target_ref.shape[1]
    place = lax.broadcasted_iota(jnp.int32, (size, LANES), 1) // BLOCK
    first = lax.rem(place - mine + count, count) < count // 2
    for c in range(count):
        at = c * chunk
        target_ref[c] = jnp.where(
            first, narrow[at : at + size, :], narrow[at + half : at + half + size, :]
        )
    out.append(pltpu.make_async_copy(target_ref, target_out, sems.at[1]))
    out[1].start()
    for copy in out:
        copy.wait()


def spread(tiles):
    count = len(tiles)
    lane = lax.broadcasted_iota(jnp.int32, tiles[0].shape, 1) // BLOCK
    tiles = [tiles[(count - t) % count] for t in range(count)]
    bit = 1
    while bit < count:
        upper = (lane & bit) != 0
        tiles = [jnp.where(upper, tiles[t - bit], tiles[t]) for t in range(count)]
        bit *= 2
    return tiles


def gathered(tiles):
    return [
        z if t == 0 else pltpu.roll(z, LANES - BLOCK * t, 1) for t, z in enumerate(spread(tiles))
    ]


def scattered(tiles):
    return spread([x if t == 0 else pltpu.roll(x, BLOCK * t, 1) for t, x in enumerate(tiles)])


def times_exact(x, matrix, parts):
    total = None
    for part in range(parts):
        piece = x.astype(jnp.bfloat16)
        term = jnp.dot(piece, matrix, preferred_element_type=jnp.float32)
        total = term if total is None else total + term
        if part < parts - 1:
            x = x - piece.astype(jnp.float32)
    return total


def core_kernel(own_ref, north_ref, south_ref, target_ref, contents_out, *scratch):
    state = (scratch[0:4], scratch[4:8])
    geo, place, result, spin, out_ref, sem = scratch[8:14]
    count, width, _ = own_ref.shape
    chunk = out_ref.shape[1]
    half = chunk // 2
    rim = (width - chunk) // 2
    lat = lax.axis_index("lat")
    lat_rows = lax.axis_size("lat") * 4
    rows = 12

    for i in range(target_ref.shape[1] // BLOCK):
        at = pl.ds(i * BLOCK, BLOCK)
        tiles = gathered([target_ref[s, at, :] for s in range(count)])
        keep = min(BLOCK, half - i * BLOCK)
        for j in range(2):
            for k in range(8):
                start = j * half + i * BLOCK
                place[k, start : start + keep, :] = tiles[8 * j + k][:keep]

    def unpack(i, carry):
        at = pl.ds(pl.multiple_of(i * BLOCK, BLOCK), BLOCK)
        for ref, base in ((south_ref, 0), (own_ref, 4), (north_ref, 8)):
            tiles = gathered([ref[s, at, :] for s in range(count)])
            for f in range(4):
                for r in range(4):
                    state[0][f][base + r, at, :] = tiles[4 * f + r]
        return carry

    lax.fori_loop(0, width // BLOCK, unpack, 0, unroll=2)

    row_level = lax.broadcasted_iota(jnp.int32, (LANES, LANES), 0)
    col_level = lax.broadcasted_iota(jnp.int32, (LANES, LANES), 1)
    below = jnp.where(row_level > col_level, 1.0, jnp.where(row_level == col_level, 0.5, 0.0))
    below = below.astype(jnp.bfloat16)
    above = jnp.where(row_level < col_level, 1.0, 0.0).astype(jnp.bfloat16)
    slope = 0.05 / math.sqrt(LANES)

    row_index = lax.broadcasted_iota(jnp.int32, (16, LANES), 0) + (lat * 4 - 4)
    angle = math.pi * ((row_index.astype(jnp.float32) + 0.5) / lat_rows - 0.5)
    spin[...] = 0.15 * jnp.sin(angle)

    def east(x):
        return pltpu.roll(x, width - 1, 0)

    def west(x):
        return pltpu.roll(x, 1, 0)

    def upwind(speed, behind, ahead):
        return speed * jnp.where(speed > 0.0, behind, ahead)

    for step in range(STEPS):
        u_ref, v_ref, t_ref, d_ref = state[step % 2]
        new = state[1 - step % 2]
        size = rows - 2 * step
        load = d_ref[step : rows - step] * t_ref[step : rows - step]
        heights = slope * times_exact(load.reshape(size * width, LANES), below, 3)
        geo[step : rows - step] = heights.reshape(size, width, LANES)

        def advance(j, flux_down):
            u, v, t, d = u_ref[j], v_ref[j], t_ref[j], d_ref[j]
            v_n, d_n = v_ref[j + 1], d_ref[j + 1]
            g = geo[j]
            cor = spin[pl.ds(j, 1), :]
            flux_x = upwind(u + east(u), d, east(d))
            flux_up = upwind(v + v_n, d, d_n)
            new[0][j] = u - (east(g) - west(g)) + cor * v
            new[1][j] = v - (geo[j + 1] - geo[j - 1]) - cor * u
            new[2][j] = t - 0.05 * (
                u * (east(t) - west(t)) + v * (t_ref[j + 1] - t_ref[j - 1])
            )
            new[3][j] = d - 0.05 * (flux_x - west(flux_x) + flux_up - flux_down)
            return flux_up

        first = step + 1
        flux_start = upwind(v_ref[step] + v_ref[first], d_ref[step], d_ref[first])
        lax.fori_loop(first, rows - first, advance, flux_start, unroll=2)

        if first < 4:

            @pl.when(lat == 0)
            def _():
                for ref in new[1:]:
                    ref[:4] = jnp.zeros((4, width, LANES), jnp.float32)

            @pl.when(lat == lax.axis_size("lat") - 1)
            def _():
                for ref in new[1:]:
                    ref[8:] = jnp.zeros((4, width, LANES), jnp.float32)

    u, v, t, d = (ref[4:8, rim : rim + chunk, :] for ref in state[STEPS % 2])
    for f, q in enumerate((u * d, v * d, t * d, d)):
        result[4 * f : 4 * f + 4] = q
    flat = result[...].reshape(count * chunk, LANES)
    geo_rows = times_exact(flat, above, 3).reshape(count, chunk, LANES)
    lane = lax.broadcasted_iota(jnp.int32, (chunk, LANES), 1)
    for r in range(4):
        source = place[4 + r].astype(jnp.int32)
        part = place[r]
        for f in range(4):
            k = 4 * f + r
            mass = jnp.take_along_axis(geo_rows[k], source, axis=1) + part * jnp.take_along_axis(
                result[k], source, axis=1
            )
            result[k] = mass - jnp.where(lane == 0, 0.0, pltpu.roll(mass, 1, 1))

    def pack(i, carry):
        at = pl.ds(pl.multiple_of(i * BLOCK, BLOCK), BLOCK)
        for s, tile in enumerate(scattered([result[k, at, :] for k in range(count)])):
            out_ref[s, at, :] = tile
        return carry

    lax.fori_loop(0, chunk // BLOCK, pack, 0, unroll=3)
    copy = pltpu.make_async_copy(out_ref, contents_out, sem)
    copy.start()
    copy.wait()


def receive_kernel(in_ref, *refs):
    outs, turned = refs[:4], refs[4]
    rows, _, lon = outs[0].shape
    count = in_ref.shape[0]
    mine = lax.axis_index("lev")
    flat = in_ref[...].reshape(lon, LANES)
    for at in range(0, lon, LANES):
        turned[:, :, at : at + LANES] = flat[at : at + LANES, :].T.reshape(count, BLOCK, LANES)
    for f, ref in enumerate(outs):
        for r in range(rows):
            ref[r] = turned[lax.rem(mine + rows * f + r, count)]


def call(kernel, ins, outs, scratch, *args):
    shapes = [jax.ShapeDtypeStruct(shape, jnp.float32) for shape, _ in outs]
    return pl.pallas_call(
        kernel,
        out_shape=shapes,
        in_specs=[pl.BlockSpec(memory_space=ins)] * len(args),
        out_specs=[pl.BlockSpec(memory_space=space) for _, space in outs],
        scratch_shapes=[
            pltpu.VMEM(shape, jnp.float32) if isinstance(shape, tuple) else shape
            for shape in scratch
        ],
        compiler_params=pltpu.CompilerParams(vmem_limit_bytes=40 * 2**20),
    )(*args)


def body(wind_east, wind_north, pot_temp, thickness, source_level, fraction):
    rows, depth, lon = wind_east.shape
    count = lax.axis_size("lev")
    blocks = lax.axis_size("lat")
    chunk = lon // count
    width = chunk + 2 * STEPS
    size = -(-(chunk // 2) // BLOCK) * BLOCK
    slab = wind_east.shape
    stack = (count, depth, lon)
    state, target = call(
        send_kernel,
        pltpu.HBM,
        [((count, width, LANES), pltpu.HBM), ((count, size, LANES), pltpu.HBM)],
        [slab] * 5
        + [pltpu.VMEM(slab, jnp.int32)]
        + [stack, stack, (lon + 2 * BLOCK, LANES), (lon + BLOCK, LANES)]
        + [(count, width, LANES), (count, size, LANES), pltpu.SemaphoreType.DMA((6,))],
        wind_east, wind_north, pot_temp, thickness, fraction, source_level,
    )
    own = lax.all_to_all(state, "lev", 0, 0, tiled=True)
    north = lax.ppermute(own, "lat", [(i + 1, i) for i in range(blocks - 1)])
    south = lax.ppermute(own, "lat", [(i, i + 1) for i in range(blocks - 1)])
    own, target = lax.optimization_barrier((own, target))
    target = lax.all_to_all(target, "lev", 0, 0, tiled=True)
    (contents,) = call(
        core_kernel,
        pltpu.VMEM,
        [((count, chunk, LANES), pltpu.HBM)],
        [(3 * rows, width, LANES)] * 9
        + [(8, chunk, LANES), (count, chunk, LANES), (16, LANES), (count, chunk, LANES)]
        + [pltpu.SemaphoreType.DMA],
        own, north, south, target,
    )
    contents = lax.all_to_all(contents, "lev", 0, 0, tiled=True)
    return tuple(
        call(receive_kernel, pltpu.VMEM, [(slab, pltpu.VMEM)] * 4, [stack], contents)
    )


def solution(mesh):
    placed = P("lat", "lev", None)
    return jax.shard_map(
        body, mesh=mesh, in_specs=(placed,) * 6, out_specs=(placed,) * 4, check_vma=False
    )
```

time: 100 us -> 90.4 us (0.904)
  Pallas kernels: 18.9 us -> 9.21 us
    pallas_call x3, Pallas kernels: 18.9 us -> 9.21 us  [call(): pl.pallas_call(kernel, out_shape=shapes, in_specs=[pl.BlockSpec(memory_sp...]
where the time goes in v2:
time: 90.4 us; the launch traced here: 90 us
  blocking collectives  69.1 us (76%)
  Pallas kernels  9.21 us (10%)
  starting transfers between devices  5.55 us (6%)
  local copies, waits for them, and re-layouts  5.45 us (6%)
    all_to_all x1, blocking collectives, body(): own = lax.all_to_all(state, 'lev', 0, 0, tiled=True)  28.8 us
    all_to_all x1, blocking collectives, body(): contents = lax.all_to_all(contents, 'lev', 0, 0, tiled=True)  24.2 us
    all_to_all x1, blocking collectives, body(): target = lax.all_to_all(target, 'lev', 0, 0, tiled=True)  16.1 us
    pallas_call x3, Pallas kernels, call(): pl.pallas_call(kernel, out_shape=shapes, in_specs=[pl.BlockSpec(memory_sp...  9.21 us
    unnamed x12, local copies, waits for them, and re-layouts  5.45 us
    ppermute x1, starting transfers between devices, body(): north = lax.ppermute(own, 'lat', [(i + 1, i) for i in range(blocks - 1)])  3.64 us
    ppermute x1, starting transfers between devices, body(): south = lax.ppermute(own, 'lat', [(i, i + 1) for i in range(blocks - 1)])  1.91 us
  transfers between devices with their start and end apart: 2, of which 0 were waited for; matrix products, arithmetic and copies ran while one was open for 0% of the time, Pallas kernels for 0%

profile of v2, /device:TPU:192, one launch (start us, length us, event | category | flops | bytes accessed | tf_op | source)
XLA Modules:
  0.0 90.0 jit_solution(1229387808360542205)
XLA Ops:
  0.6 0.0 copy-start
  0.6 0.9 %copy-done = f32[4,8,1152]{2,1,0:T(8,128)S(1)} copy-done((f32[4,8,1152]{2,1,0:T(8,128)S(1)}, f32[4,8,1152]{2,1,0:T(8,128)}, u32[]{:S(2)}) %copy-start) | copy-done | bytes 147480
  1.5 0.0 copy-start.1
  1.5 0.9 %copy-done.1 = f32[4,8,1152]{2,1,0:T(8,128)S(1)} copy-done((f32[4,8,1152]{2,1,0:T(8,128)S(1)}, f32[4,8,1152]{2,1,0:T(8,128)}, u32[]{:S(2)}) %copy-start.1) | copy-done | bytes 147480
  2.5 0.0 copy-start.2
  2.5 0.9 %copy-done.2 = f32[4,8,1152]{2,1,0:T(8,128)S(1)} copy-done((f32[4,8,1152]{2,1,0:T(8,128)S(1)}, f32[4,8,1152]{2,1,0:T(8,128)}, u32[]{:S(2)}) %copy-start.2) | copy-done | bytes 147480
  3.4 0.0 copy-start.3
  3.4 0.9 %copy-done.3 = f32[4,8,1152]{2,1,0:T(8,128)S(1)} copy-done((f32[4,8,1152]{2,1,0:T(8,128)S(1)}, f32[4,8,1152]{2,1,0:T(8,128)}, u32[]{:S(2)}) %copy-start.3) | copy-done | bytes 147480
  4.3 0.0 copy-start.4
  4.3 0.9 %copy-done.4 = f32[4,8,1152]{2,1,0:T(8,128)S(1)} copy-done((f32[4,8,1152]{2,1,0:T(8,128)S(1)}, f32[4,8,1152]{2,1,0:T(8,128)}, u32[]{:S(2)}) %copy-start.4) | copy-done | bytes 147480
  5.2 0.0 copy-start.5
  5.2 0.9 %copy-done.5 = s32[4,8,1152]{2,1,0:T(8,128)S(1)} copy-done((s32[4,8,1152]{2,1,0:T(8,128)S(1)}, s32[4,8,1152]{2,1,0:T(8,128)}, u32[]{:S(2)}) %copy-start.5) | copy-done | bytes 147480
  6.1 2.2 %shard_map.93 = (f32[16,80,128]{2,1,0:T(8,128)S(1)}, f32[16,40,128]{2,1,0:T(8,128)S(1)}) custom-call(f32[4,8,1152]{2,1,0:T(8,128)S(1)} %copy-done, f32[4,8,1152]{2,1,0:T(8,128)S(1)} %copy-done.1, f32[4,8,1152]{2,1,0:T(8,128)S(1)} %copy-done.2, f32[4,8,1152]{2,1,0:T(8,128)S(1)} %copy-done.3, f32[4,8,1152]{2,1,0:T(8,128)S(1)} %copy-done.4, ...), custom_call_target="tpu_custom_call" | custom-call | tf_op jit(solution)/shard_map/pallas_call | solution.py:241
  8.3 28.8 %all_to_all.15.own_ref = f32[16,80,128]{2,1,0:T(8,128)S(1)} all-to-all(f32[16,80,128]{2,1,0:T(8,128)S(1)} %get-tuple-element.8), channel_id=1, replica_groups=mesh['lat'=32,'lev'=16] {'lev'}, dimensions={0} | all-to-all | bytes 1310720 | tf_op jit(solution)/shard_map/all_to_all | solution.py:273
  37.1 1.9 %collective-permute-start.1 = (f32[16,80,128]{2,1,0:T(8,128)S(1)}, f32[16,80,128]{2,1,0:T(8,128)S(1)}, u32[]{:S(2)}, u32[]{:S(2)}) collective-permute-start(f32[16,80,128]{2,1,0:T(8,128)S(1)} %all_to_all.15.own_ref), channel_id=1, source_target_pairs={{0,16},{16,32},{32,48},{48,64},{64,80},{80,96},{96,112},{112,128},... | collective-permute-start | bytes 1966088 | tf_op jit(solution)/shard_map/ppermute | solution.py:275
  39.0 3.6 %collective-permute-start = (f32[16,80,128]{2,1,0:T(8,128)S(1)}, f32[16,80,128]{2,1,0:T(8,128)S(1)}, u32[]{:S(2)}, u32[]{:S(2)}) collective-permute-start(f32[16,80,128]{2,1,0:T(8,128)S(1)} %all_to_all.15.own_ref), channel_id=1, source_target_pairs={{16,0},{32,16},{48,32},{64,48},{80,64},{96,80},{112,96},{128,112},... | collective-permute-start | bytes 1966088 | tf_op jit(solution)/shard_map/ppermute | solution.py:274
  42.6 16.1 %all_to_all.16.target_ref = f32[16,40,128]{2,1,0:T(8,128)S(1)} all-to-all(f32[16,40,128]{2,1,0:T(8,128)S(1)} %get-tuple-element.11), channel_id=1, replica_groups=mesh['lat'=32,'lev'=16] {'lev'}, dimensions={0} | all-to-all | bytes 655360 | tf_op jit(solution)/shard_map/all_to_all | solution.py:277
  58.8 0.0 collective-permute-done.1.south_ref
  58.8 0.0 collective-permute-done.north_ref
  58.8 6.0 %shard_map.94 = f32[16,72,128]{2,1,0:T(8,128)S(1)} custom-call(f32[16,80,128]{2,1,0:T(8,128)S(1)} %all_to_all.15.own_ref, f32[16,80,128]{2,1,0:T(8,128)S(1)} %collective-permute-done.north_ref, f32[16,80,128]{2,1,0:T(8,128)S(1)} %collective-permute-done.1.south_ref, f32[16,40,128]{2,1,0:T(8,128)S(1)} %all_to_all.16.target_ref), custom_call_target="tpu_custom_call" | custom-call | tf_op jit(solution)/shard_map/pallas_call | solution.py:241
  64.7 24.2 %all_to_all.17.in_ref = f32[16,72,128]{2,1,0:T(8,128)S(1)} all-to-all(f32[16,72,128]{2,1,0:T(8,128)S(1)} %shard_map.94), channel_id=1, replica_groups=mesh['lat'=32,'lev'=16] {'lev'}, dimensions={0} | all-to-all | bytes 1179648 | tf_op jit(solution)/shard_map/all_to_all | solution.py:287
  88.9 1.1 %shard_map.95 = (f32[4,8,1152]{2,1,0:T(8,128)}, f32[4,8,1152]{2,1,0:T(8,128)}, f32[4,8,1152]{2,1,0:T(8,128)}, f32[4,8,1152]{2,1,0:T(8,128)}) custom-call(f32[16,72,128]{2,1,0:T(8,128)S(1)} %all_to_all.17.in_ref), custom_call_target="tpu_custom_call" | custom-call | tf_op jit(solution)/shard_map/pallas_call | solution.py:241
Async XLA Ops:
  0.6 0.9 %copy-start = (f32[4,8,1152]{2,1,0:T(8,128)S(1)}, f32[4,8,1152]{2,1,0:T(8,128)}, u32[]{:S(2)}) copy-start(f32[4,8,1152]{2,1,0:T(8,128)} %u_in.1) | copy-start | bytes 442372
  1.5 0.9 %copy-start.1 = (f32[4,8,1152]{2,1,0:T(8,128)S(1)}, f32[4,8,1152]{2,1,0:T(8,128)}, u32[]{:S(2)}) copy-start(f32[4,8,1152]{2,1,0:T(8,128)} %v_in.1) | copy-start | bytes 442372
  2.5 0.9 %copy-start.2 = (f32[4,8,1152]{2,1,0:T(8,128)S(1)}, f32[4,8,1152]{2,1,0:T(8,128)}, u32[]{:S(2)}) copy-start(f32[4,8,1152]{2,1,0:T(8,128)} %t_in.1) | copy-start | bytes 442372
  3.4 0.9 %copy-start.3 = (f32[4,8,1152]{2,1,0:T(8,128)S(1)}, f32[4,8,1152]{2,1,0:T(8,128)}, u32[]{:S(2)}) copy-start(f32[4,8,1152]{2,1,0:T(8,128)} %d_in.1) | copy-start | bytes 442372
  4.3 0.9 %copy-start.4 = (f32[4,8,1152]{2,1,0:T(8,128)S(1)}, f32[4,8,1152]{2,1,0:T(8,128)}, u32[]{:S(2)}) copy-start(f32[4,8,1152]{2,1,0:T(8,128)} %f_in.1) | copy-start | bytes 442372
  5.2 0.9 %copy-start.5 = (s32[4,8,1152]{2,1,0:T(8,128)S(1)}, s32[4,8,1152]{2,1,0:T(8,128)}, u32[]{:S(2)}) copy-start(s32[4,8,1152]{2,1,0:T(8,128)} %s_in.1) | copy-start | bytes 442372
  37.1 21.7 %collective-permute-start.1 = (f32[16,80,128]{2,1,0:T(8,128)S(1)}, f32[16,80,128]{2,1,0:T(8,128)S(1)}, u32[]{:S(2)}, u32[]{:S(2)}) collective-permute-start(f32[16,80,128]{2,1,0:T(8,128)S(1)} %all_to_all.15.own_ref), channel_id=1, source_target_pairs={{0,16},{16,32},{32,48},{48,64},{64,80},{80,96},{96,112},{112,128},... | collective-permute-start | bytes 1966088 | tf_op jit(solution)/shard_map/ppermute | solution.py:275
  39.0 19.8 %collective-permute-start = (f32[16,80,128]{2,1,0:T(8,128)S(1)}, f32[16,80,128]{2,1,0:T(8,128)S(1)}, u32[]{:S(2)}, u32[]{:S(2)}) collective-permute-start(f32[16,80,128]{2,1,0:T(8,128)S(1)} %all_to_all.15.own_ref), channel_id=1, source_target_pairs={{16,0},{32,16},{48,32},{64,48},{80,64},{96,80},{112,96},{128,112},... | collective-permute-start | bytes 1966088 | tf_op jit(solution)/shard_map/ppermute | solution.py:274

commit v3 on v2

--- a/solution.py
+++ b/solution.py
@@ -12,64 +12,65 @@
 BLOCK = 8
 
 
-def send_kernel(u_in, v_in, t_in, d_in, f_in, s_in, state_out, target_out, *scratch):
-    fields, levels = scratch[:5], scratch[5]
-    wide_stack, narrow_stack, wide, narrow, state_ref, target_ref, sems = scratch[6:]
+def fetch(sources, targets, sems):
+    copies = [
+        pltpu.make_async_copy(source, target, sems.at[i])
+        for i, (source, target) in enumerate(zip(sources, targets))
+    ]
+    for copy in copies:
+        copy.start()
+    return copies
+
+
+def turn(stack, flat, base):
+    lon = stack.shape[-1]
+    for at in range(0, lon, LANES):
+        flat[base + at : base + at + LANES, :] = (
+            stack[:, :, at : at + LANES].reshape(LANES, LANES).T
+        )
+
+
+def send_state(u_in, v_in, t_in, d_in, state_ref, *scratch):
+    fields, (stack, flat, sems) = scratch[:4], scratch[4:]
     rows, _, lon = u_in.shape
     count, width, _ = state_ref.shape
     chunk = lon // count
-    half = chunk // 2
     rim = (width - chunk) // 2
     mine = lax.axis_index("lev")
-    copies = [
-        pltpu.make_async_copy(source, target, sems.at[i])
-        for i, (source, target) in enumerate(
-            zip((u_in, v_in, t_in, d_in, f_in, s_in), fields + (levels,))
-        )
-    ]
-    for copy in copies:
-        copy.start()
-
-    def block(j):
-        return lax.rem(mine + j, count)
-
+    copies = fetch((u_in, v_in, t_in, d_in), fields, sems)
     for f in range(4):
         copies[f].wait()
         for r in range(rows):
-            wide_stack[block(rows * f + r)] = fields[f][r]
-    for at in range(0, lon, LANES):
-        wide[BLOCK + at : BLOCK + at + LANES, :] = (
-            wide_stack[:, :, at : at + LANES].reshape(LANES, LANES).T
-        )
-    wide[:BLOCK, :] = wide[lon : lon + BLOCK, :]
-    wide[lon + BLOCK :, :] = wide[BLOCK : 2 * BLOCK, :]
+            stack[lax.rem(mine + rows * f + r, count)] = fields[f][r]
+    turn(stack, flat, BLOCK)
+    flat[:BLOCK, :] = flat[lon : lon + BLOCK, :]
+    flat[lon + BLOCK :, :] = flat[BLOCK : 2 * BLOCK, :]
     for c in range(count):
         at = BLOCK + c * chunk - rim
-        state_ref[c] = wide[at : at + width, :]
-    out = [pltpu.make_async_copy(state_ref, state_out, sems.at[0])]
-    out[0].start()
-
-    copies[4].wait()
-    copies[5].wait()
+        state_ref[c] = flat[at : at + width, :]
+
+
+def send_target(f_in, s_in, target_ref, part, level, stack, flat, sems):
+    rows, _, lon = f_in.shape
+    count, size, _ = target_ref.shape
+    chunk = lon // count
+    half = chunk // 2
+    mine = lax.axis_index("lev")
+    for copy in fetch((f_in, s_in), (part, level), sems):
+        copy.wait()
     for h in range(2):
         for r in range(rows):
-            narrow_stack[block(8 * h + r)] = fields[4][r]
-            narrow_stack[block(8 * h + 4 + r)] = levels[r].astype(jnp.float32)
-    for at in range(0, lon, LANES):
-        narrow[at : at + LANES, :] = narrow_stack[:, :, at : at + LANES].reshape(LANES, LANES).T
-    narrow[lon:, :] = jnp.zeros((narrow.shape[0] - lon, LANES), jnp.float32)
-    size = target_ref.shape[1]
+            stack[lax.rem(mine + 8 * h + r, count)] = part[r]
+            stack[lax.rem(mine + 8 * h + 4 + r, count)] = level[r].astype(jnp.float32)
+    turn(stack, flat, 0)
+    flat[lon:, :] = jnp.zeros((flat.shape[0] - lon, LANES), jnp.float32)
     place = lax.broadcasted_iota(jnp.int32, (size, LANES), 1) // BLOCK
     first = lax.rem(place - mine + count, count) < count // 2
     for c in range(count):
         at = c * chunk
         target_ref[c] = jnp.where(
-            first, narrow[at : at + size, :], narrow[at + half : at + half + size, :]
+            first, flat[at : at + size, :], flat[at + half : at + half + size, :]
         )
-    out.append(pltpu.make_async_copy(target_ref, target_out, sems.at[1]))
-    out[1].start()
-    for copy in out:
-        copy.wait()
 
 
 def spread(tiles):
@@ -105,25 +106,15 @@
     return total
 
 
-def core_kernel(own_ref, north_ref, south_ref, target_ref, contents_out, *scratch):
+def step_kernel(own_ref, north_ref, south_ref, contents_ref, prefix_ref, *scratch):
     state = (scratch[0:4], scratch[4:8])
-    geo, place, result, spin, out_ref, sem = scratch[8:14]
+    geo, spin = scratch[8:10]
     count, width, _ = own_ref.shape
-    chunk = out_ref.shape[1]
-    half = chunk // 2
+    chunk = contents_ref.shape[1]
     rim = (width - chunk) // 2
     lat = lax.axis_index("lat")
     lat_rows = lax.axis_size("lat") * 4
     rows = 12
-
-    for i in range(target_ref.shape[1] // BLOCK):
-        at = pl.ds(i * BLOCK, BLOCK)
-        tiles = gathered([target_ref[s, at, :] for s in range(count)])
-        keep = min(BLOCK, half - i * BLOCK)
-        for j in range(2):
-            for k in range(8):
-                start = j * half + i * BLOCK
-                place[k, start : start + keep, :] = tiles[8 * j + k][:keep]
 
     def unpack(i, carry):
         at = pl.ds(pl.multiple_of(i * BLOCK, BLOCK), BLOCK)
@@ -197,18 +188,31 @@
 
     u, v, t, d = (ref[4:8, rim : rim + chunk, :] for ref in state[STEPS % 2])
     for f, q in enumerate((u * d, v * d, t * d, d)):
-        result[4 * f : 4 * f + 4] = q
-    flat = result[...].reshape(count * chunk, LANES)
-    geo_rows = times_exact(flat, above, 3).reshape(count, chunk, LANES)
+        contents_ref[4 * f : 4 * f + 4] = q
+    flat = contents_ref[...].reshape(count * chunk, LANES)
+    prefix_ref[...] = times_exact(flat, above, 3).reshape(count, chunk, LANES)
+
+
+def remap_kernel(target_ref, contents_ref, prefix_ref, out_ref, place, result):
+    count, chunk, _ = contents_ref.shape
+    half = chunk // 2
+    for i in range(target_ref.shape[1] // BLOCK):
+        at = pl.ds(i * BLOCK, BLOCK)
+        tiles = gathered([target_ref[s, at, :] for s in range(count)])
+        keep = min(BLOCK, half - i * BLOCK)
+        for j in range(2):
+            for k in range(8):
+                start = j * half + i * BLOCK
+                place[k, start : start + keep, :] = tiles[8 * j + k][:keep]
     lane = lax.broadcasted_iota(jnp.int32, (chunk, LANES), 1)
     for r in range(4):
         source = place[4 + r].astype(jnp.int32)
         part = place[r]
         for f in range(4):
             k = 4 * f + r
-            mass = jnp.take_along_axis(geo_rows[k], source, axis=1) + part * jnp.take_along_axis(
-                result[k], source, axis=1
-            )
+            mass = jnp.take_along_axis(
+                prefix_ref[k], source, axis=1
+            ) + part * jnp.take_along_axis(contents_ref[k], source, axis=1)
             result[k] = mass - jnp.where(lane == 0, 0.0, pltpu.roll(mass, 1, 1))
 
     def pack(i, carry):
@@ -218,9 +222,6 @@
         return carry
 
     lax.fori_loop(0, chunk // BLOCK, pack, 0, unroll=3)
-    copy = pltpu.make_async_copy(out_ref, contents_out, sem)
-    copy.start()
-    copy.wait()
 
 
 def receive_kernel(in_ref, *refs):
@@ -236,18 +237,20 @@
             ref[r] = turned[lax.rem(mine + rows * f + r, count)]
 
 
-def call(kernel, ins, outs, scratch, *args):
-    shapes = [jax.ShapeDtypeStruct(shape, jnp.float32) for shape, _ in outs]
+def call(kernel, ins, outs, scratch, *args, limit=40 * 2**20, flops=0):
+    shapes = [jax.ShapeDtypeStruct(shape, jnp.float32) for shape in outs]
+    moved = sum(4 * math.prod(a.shape) for a in (*args, *shapes))
     return pl.pallas_call(
         kernel,
         out_shape=shapes,
         in_specs=[pl.BlockSpec(memory_space=ins)] * len(args),
-        out_specs=[pl.BlockSpec(memory_space=space) for _, space in outs],
+        out_specs=[pl.BlockSpec(memory_space=pltpu.VMEM)] * len(outs),
         scratch_shapes=[
             pltpu.VMEM(shape, jnp.float32) if isinstance(shape, tuple) else shape
             for shape in scratch
         ],
-        compiler_params=pltpu.CompilerParams(vmem_limit_bytes=40 * 2**20),
+        cost_estimate=pl.CostEstimate(flops=flops, bytes_accessed=moved, transcendentals=0),
+        compiler_params=pltpu.CompilerParams(vmem_limit_bytes=limit),
     )(*args)
 
 
@@ -260,34 +263,34 @@
     size = -(-(chunk // 2) // BLOCK) * BLOCK
     slab = wind_east.shape
     stack = (count, depth, lon)
-    state, target = call(
-        send_kernel,
-        pltpu.HBM,
-        [((count, width, LANES), pltpu.HBM), ((count, size, LANES), pltpu.HBM)],
-        [slab] * 5
-        + [pltpu.VMEM(slab, jnp.int32)]
-        + [stack, stack, (lon + 2 * BLOCK, LANES), (lon + BLOCK, LANES)]
-        + [(count, width, LANES), (count, size, LANES), pltpu.SemaphoreType.DMA((6,))],
-        wind_east, wind_north, pot_temp, thickness, fraction, source_level,
+    column = (count, chunk, LANES)
+    (state,) = call(
+        send_state, pltpu.HBM, [(count, width, LANES)],
+        [slab] * 4 + [stack, (lon + 2 * BLOCK, LANES), pltpu.SemaphoreType.DMA((4,))],
+        wind_east, wind_north, pot_temp, thickness, limit=60 * 2**20,
+    )
+    (target,) = call(
+        send_target, pltpu.HBM, [(count, size, LANES)],
+        [slab, pltpu.VMEM(slab, jnp.int32), stack, (lon + BLOCK, LANES)]
+        + [pltpu.SemaphoreType.DMA((2,))],
+        fraction, source_level, limit=60 * 2**20,
     )
     own = lax.all_to_all(state, "lev", 0, 0, tiled=True)
+    own, target = lax.optimization_barrier((own, target))
     north = lax.ppermute(own, "lat", [(i + 1, i) for i in range(blocks - 1)])
     south = lax.ppermute(own, "lat", [(i, i + 1) for i in range(blocks - 1)])
-    own, target = lax.optimization_barrier((own, target))
     target = lax.all_to_all(target, "lev", 0, 0, tiled=True)
+    contents, prefix = call(
+        step_kernel, pltpu.VMEM, [column] * 2,
+        [(3 * rows, width, LANES)] * 9 + [(16, LANES)],
+        own, north, south, flops=3 * 10**8,
+    )
     (contents,) = call(
-        core_kernel,
-        pltpu.VMEM,
-        [((count, chunk, LANES), pltpu.HBM)],
-        [(3 * rows, width, LANES)] * 9
-        + [(8, chunk, LANES), (count, chunk, LANES), (16, LANES), (count, chunk, LANES)]
-        + [pltpu.SemaphoreType.DMA],
-        own, north, south, target,
+        remap_kernel, pltpu.VMEM, [column], [(8, chunk, LANES), column],
+        target, contents, prefix,
     )
     contents = lax.all_to_all(contents, "lev", 0, 0, tiled=True)
-    return tuple(
-        call(receive_kernel, pltpu.VMEM, [(slab, pltpu.VMEM)] * 4, [stack], contents)
-    )
+    return tuple(call(receive_kernel, pltpu.VMEM, [slab] * 4, [stack], contents))
 
 
 def solution(mesh):

time: 90.4 us -> 81.9 us (0.906)
  blocking collectives: 69.1 us -> 24.2 us
  waiting for transfers between devices: 0.01 us -> 26.9 us
  starting transfers between devices: 5.55 us -> 17.2 us
  local copies, waits for them, and re-layouts: 5.45 us -> 0 us
  Pallas kernels: 9.21 us -> 12.4 us
    all_to_all x2 -> x0, blocking collectives: 44.9 us -> none  [the longest x1 28.8 us: body(): own = lax.all_to_all(state, 'lev', 0, 0, tiled=True)]
    all_to_all x0 -> x2, waiting for transfers between devices: none -> 22.4 us  [the longest x1 18.1 us: body(): own = lax.all_to_all(state, 'lev', 0, 0, tiled=True)]
    all_to_all x0 -> x2, starting transfers between devices: none -> 11.7 us  [the longest x1 8.14 us: body(): own = lax.all_to_all(state, 'lev', 0, 0, tiled=True)]
    unnamed x12 -> x0, local copies, waits for them, and re-layouts: 5.45 us -> none
    pallas_call x3 -> x5, Pallas kernels: 9.21 us -> 12.4 us  [call(): pl.pallas_call(kernel, out_shape=shapes, in_specs=[pl.BlockSpec(memory_sp...]
    ppermute x1, waiting for transfers between devices: 0.01 us -> 2.76 us  [body(): south = lax.ppermute(own, 'lat', [(i, i + 1) for i in range(blocks - 1)])]
    ppermute x1, waiting for transfers between devices: 0.01 us -> 1.76 us  [body(): north = lax.ppermute(own, 'lat', [(i + 1, i) for i in range(blocks - 1)])]
  transfers between devices with their start and end apart: 2 -> 4, of which waited for: 0 -> 4; matrix products, arithmetic and copies ran while one was open for 0% -> 0% of each run, Pallas kernels for 0% -> 8%
where the time goes in v3:
time: 81.9 us; the launch traced here: 81.5 us
  waiting for transfers between devices  26.9 us (33%)
  blocking collectives  24.2 us (30%)
  starting transfers between devices  17.2 us (21%)
  Pallas kernels  12.4 us (15%)
    all_to_all x1, blocking collectives, body(): contents = lax.all_to_all(contents, 'lev', 0, 0, tiled=True)  24.2 us
    all_to_all x1, waiting for transfers between devices, body(): own = lax.all_to_all(state, 'lev', 0, 0, tiled=True)  18.1 us
    pallas_call x5, Pallas kernels, call(): pl.pallas_call(kernel, out_shape=shapes, in_specs=[pl.BlockSpec(memory_sp...  12.4 us
    all_to_all x1, starting transfers between devices, body(): own = lax.all_to_all(state, 'lev', 0, 0, tiled=True)  8.14 us
    all_to_all x1, waiting for transfers between devices, body(): target = lax.all_to_all(target, 'lev', 0, 0, tiled=True)  4.28 us
    ppermute x1, starting transfers between devices, body(): north = lax.ppermute(own, 'lat', [(i + 1, i) for i in range(blocks - 1)])  3.64 us
    all_to_all x1, starting transfers between devices, body(): target = lax.all_to_all(target, 'lev', 0, 0, tiled=True)  3.55 us
    ppermute x1, waiting for transfers between devices, body(): south = lax.ppermute(own, 'lat', [(i, i + 1) for i in range(blocks - 1)])  2.76 us
  transfers between devices with their start and end apart: 4, of which 4 were waited for; matrix products, arithmetic and copies ran while one was open for 0% of the time, Pallas kernels for 8%

profile of v3, /device:TPU:192, one launch (start us, length us, event | category | flops | bytes accessed | tf_op | source)
XLA Modules:
  0.0 81.5 jit_solution(2792000937486699343)
XLA Ops:
  0.6 2.3 %shard_map.93 = f32[16,80,128]{2,1,0:T(8,128)} custom-call(f32[4,8,1152]{2,1,0:T(8,128)} %u_in.1, f32[4,8,1152]{2,1,0:T(8,128)} %v_in.1, f32[4,8,1152]{2,1,0:T(8,128)} %t_in.1, f32[4,8,1152]{2,1,0:T(8,128)} %d_in.1), custom_call_target="tpu_custom_call" | custom-call | bytes 1245184 | tf_op jit(solution)/shard_map/pallas_call | solution.py:243
  3.0 8.1 %all-to-all-start = ((f32[16,80,128]{2,1,0:T(8,128)}), f32[16,80,128]{2,1,0:T(8,128)S(1)}, u32[]{:S(2)}, u32[]{:S(2)}) async-start(f32[16,80,128]{2,1,0:T(8,128)} %shard_map.93), calls=%async_computation | async-start | bytes 1310720 | tf_op jit(solution)/shard_map/all_to_all | solution.py:278
  11.1 2.1 %shard_map.94 = f32[16,40,128]{2,1,0:T(8,128)} custom-call(f32[4,8,1152]{2,1,0:T(8,128)} %f_in.1, s32[4,8,1152]{2,1,0:T(8,128)} %s_in.1), custom_call_target="tpu_custom_call" | custom-call | bytes 622592 | tf_op jit(solution)/shard_map/pallas_call | solution.py:243
  13.2 18.1 %all-to-all-done.own_ref = f32[16,80,128]{2,1,0:T(8,128)S(1)} async-done(((f32[16,80,128]{2,1,0:T(8,128)}), f32[16,80,128]{2,1,0:T(8,128)S(1)}, u32[]{:S(2)}, u32[]{:S(2)}) %all-to-all-start) | async-done | bytes 655392 | tf_op jit(solution)/shard_map/all_to_all | solution.py:278
  31.3 1.9 %collective-permute-start.1 = (f32[16,80,128]{2,1,0:T(8,128)S(1)}, f32[16,80,128]{2,1,0:T(8,128)S(1)}, u32[]{:S(2)}, u32[]{:S(2)}) collective-permute-start(f32[16,80,128]{2,1,0:T(8,128)S(1)} %all-to-all-done.own_ref), channel_id=1, source_target_pairs={{0,16},{16,32},{32,48},{48,64},{64,80},{80,96},{96,112},{112,128},... | collective-permute-start | bytes 1966088 | tf_op jit(solution)/shard_map/ppermute | solution.py:281
  33.2 3.6 %collective-permute-start = (f32[16,80,128]{2,1,0:T(8,128)S(1)}, f32[16,80,128]{2,1,0:T(8,128)S(1)}, u32[]{:S(2)}, u32[]{:S(2)}) collective-permute-start(f32[16,80,128]{2,1,0:T(8,128)S(1)} %all-to-all-done.own_ref), channel_id=1, source_target_pairs={{16,0},{32,16},{48,32},{64,48},{80,64},{96,80},{112,96},{128,112},... | collective-permute-start | bytes 1966088 | tf_op jit(solution)/shard_map/ppermute | solution.py:280
  36.9 3.6 %all-to-all-start.1 = ((f32[16,40,128]{2,1,0:T(8,128)}), f32[16,40,128]{2,1,0:T(8,128)S(1)}, u32[]{:S(2)}, u32[]{:S(2)}) async-start(f32[16,40,128]{2,1,0:T(8,128)} %shard_map.94), calls=%async_computation.1 | async-start | bytes 655360 | tf_op jit(solution)/shard_map/all_to_all | solution.py:282
  40.4 2.8 %collective-permute-done.1.south_ref = f32[16,80,128]{2,1,0:T(8,128)S(1)} collective-permute-done((f32[16,80,128]{2,1,0:T(8,128)S(1)}, f32[16,80,128]{2,1,0:T(8,128)S(1)}, u32[]{:S(2)}, u32[]{:S(2)}) %collective-permute-start.1) | collective-permute-done | bytes 655392 | tf_op jit(solution)/shard_map/ppermute | solution.py:281
  43.2 1.8 %collective-permute-done.north_ref = f32[16,80,128]{2,1,0:T(8,128)S(1)} collective-permute-done((f32[16,80,128]{2,1,0:T(8,128)S(1)}, f32[16,80,128]{2,1,0:T(8,128)S(1)}, u32[]{:S(2)}, u32[]{:S(2)}) %collective-permute-start) | collective-permute-done | bytes 655392 | tf_op jit(solution)/shard_map/ppermute | solution.py:280
  45.0 4.7 %shard_map.95 = (f32[16,72,128]{2,1,0:T(8,128)S(1)}, f32[16,72,128]{2,1,0:T(8,128)S(1)}) custom-call(f32[16,80,128]{2,1,0:T(8,128)S(1)} %all-to-all-done.own_ref, f32[16,80,128]{2,1,0:T(8,128)S(1)} %collective-permute-done.north_ref, f32[16,80,128]{2,1,0:T(8,128)S(1)} %collective-permute-done.1.south_ref), custom_call_target="tpu_custom_call" | custom-call | flops 300000000 | bytes 3145728 | tf_op jit(solution)/shard_map/pallas_call | solution.py:243
  49.7 4.3 %all-to-all-done.1.target_ref = f32[16,40,128]{2,1,0:T(8,128)S(1)} async-done(((f32[16,40,128]{2,1,0:T(8,128)}), f32[16,40,128]{2,1,0:T(8,128)S(1)}, u32[]{:S(2)}, u32[]{:S(2)}) %all-to-all-start.1) | async-done | bytes 327712 | tf_op jit(solution)/shard_map/all_to_all | solution.py:282
  53.9 2.3 %shard_map.96 = f32[16,72,128]{2,1,0:T(8,128)S(1)} custom-call(f32[16,40,128]{2,1,0:T(8,128)S(1)} %all-to-all-done.1.target_ref, f32[16,72,128]{2,1,0:T(8,128)S(1)} %get-tuple-element.10.contents_ref, f32[16,72,128]{2,1,0:T(8,128)S(1)} %get-tuple-element.11.prefix_ref), custom_call_target="tpu_custom_call" | custom-call | bytes 2097152 | tf_op jit(solution)/shard_map/pallas_call | solution.py:243
  56.2 24.2 %all_to_all.15.in_ref = f32[16,72,128]{2,1,0:T(8,128)S(1)} all-to-all(f32[16,72,128]{2,1,0:T(8,128)S(1)} %shard_map.96), channel_id=1, replica_groups=mesh['lat'=32,'lev'=16] {'lev'}, dimensions={0} | all-to-all | bytes 1179648 | tf_op jit(solution)/shard_map/all_to_all | solution.py:292
  80.4 1.1 %shard_map.97 = (f32[4,8,1152]{2,1,0:T(8,128)}, f32[4,8,1152]{2,1,0:T(8,128)}, f32[4,8,1152]{2,1,0:T(8,128)}, f32[4,8,1152]{2,1,0:T(8,128)}) custom-call(f32[16,72,128]{2,1,0:T(8,128)S(1)} %all_to_all.15.in_ref), custom_call_target="tpu_custom_call" | custom-call | bytes 1179648 | tf_op jit(solution)/shard_map/pallas_call | solution.py:243
Async XLA Ops:
  3.0 28.4 %all-to-all-start = ((f32[16,80,128]{2,1,0:T(8,128)}), f32[16,80,128]{2,1,0:T(8,128)S(1)}, u32[]{:S(2)}, u32[]{:S(2)}) async-start(f32[16,80,128]{2,1,0:T(8,128)} %shard_map.93), calls=%async_computation | async-start | bytes 1310720 | tf_op jit(solution)/shard_map/all_to_all | solution.py:278
  31.3 11.9 %collective-permute-start.1 = (f32[16,80,128]{2,1,0:T(8,128)S(1)}, f32[16,80,128]{2,1,0:T(8,128)S(1)}, u32[]{:S(2)}, u32[]{:S(2)}) collective-permute-start(f32[16,80,128]{2,1,0:T(8,128)S(1)} %all-to-all-done.own_ref), channel_id=1, source_target_pairs={{0,16},{16,32},{32,48},{48,64},{64,80},{80,96},{96,112},{112,128},... | collective-permute-start | bytes 1966088 | tf_op jit(solution)/shard_map/ppermute | solution.py:281
  33.2 11.7 %collective-permute-start = (f32[16,80,128]{2,1,0:T(8,128)S(1)}, f32[16,80,128]{2,1,0:T(8,128)S(1)}, u32[]{:S(2)}, u32[]{:S(2)}) collective-permute-start(f32[16,80,128]{2,1,0:T(8,128)S(1)} %all-to-all-done.own_ref), channel_id=1, source_target_pairs={{16,0},{32,16},{48,32},{64,48},{80,64},{96,80},{112,96},{128,112},... | collective-permute-start | bytes 1966088 | tf_op jit(solution)/shard_map/ppermute | solution.py:280
  36.9 17.0 %all-to-all-start.1 = ((f32[16,40,128]{2,1,0:T(8,128)}), f32[16,40,128]{2,1,0:T(8,128)S(1)}, u32[]{:S(2)}, u32[]{:S(2)}) async-start(f32[16,40,128]{2,1,0:T(8,128)} %shard_map.94), calls=%async_computation.1 | async-start | bytes 655360 | tf_op jit(solution)/shard_map/all_to_all | solution.py:282

commit v4 on v3

v4 whole, which is shorter than its diff:
```python
import math

import jax
import jax.numpy as jnp
from jax import lax
from jax.experimental import pallas as pl
from jax.experimental.pallas import tpu as pltpu
from jax.sharding import PartitionSpec as P

STEPS = 4
LANES = 128
BLOCK = 8


def slot(chunk):
    half = lax.axis_size("lat") // 2
    return chunk + lax.div(lax.axis_index("lat"), half) * (1 - 2 * (chunk % 2))


def fetch(sources, targets, sems):
    copies = [
        pltpu.make_async_copy(source, target, sems.at[i])
        for i, (source, target) in enumerate(zip(sources, targets))
    ]
    for copy in copies:
        copy.start()
    return copies


def turn(stack, flat, base):
    lon = stack.shape[-1]
    for at in range(0, lon, LANES):
        flat[base + at : base + at + LANES, :] = (
            stack[:, :, at : at + LANES].reshape(LANES, LANES).T
        )


def send_state(u_in, v_in, t_in, d_in, state_out, stack, flat, in_sems, out_sems):
    rows, _, lon = u_in.shape
    count, width, _ = state_out.shape
    chunk = lon // count
    rim = (width - chunk) // 2
    mine = lax.axis_index("lev")
    places = [stack.at[lax.rem(mine + j, count)] for j in range(4 * rows)]
    sources = [ref.at[r] for ref in (u_in, v_in, t_in, d_in) for r in range(rows)]
    for copy in fetch(sources, places, in_sems):
        copy.wait()

    base = BLOCK + rim
    outs = [
        pltpu.make_async_copy(
            flat.at[pl.ds(BLOCK + c * chunk, width)], state_out.at[slot(c)], out_sems.at[c]
        )
        for c in range(count)
    ]
    sent = 1
    for at in range(0, lon, LANES):
        flat[base + at : base + at + LANES, :] = (
            stack[:, :, at : at + LANES].reshape(LANES, LANES).T
        )
        while sent < count - 1 and (sent + 1) * chunk + rim <= at + LANES:
            outs[sent].start()
            sent += 1
    flat[base - rim : base, :] = flat[base + lon - rim : base + lon, :]
    flat[base + lon :, :] = flat[base : base + rim, :]
    outs[0].start()
    for c in range(sent, count):
        outs[c].start()
    for copy in outs:
        copy.wait()


def send_target(f_in, s_in, target_ref, part, level, stack, flat, sems):
    rows, _, lon = f_in.shape
    count, size, _ = target_ref.shape
    chunk = lon // count
    half = chunk // 2
    mine = lax.axis_index("lev")
    for copy in fetch((f_in, s_in), (part, level), sems):
        copy.wait()
    for h in range(2):
        for r in range(rows):
            stack[lax.rem(mine + 8 * h + r, count)] = part[r]
            stack[lax.rem(mine + 8 * h + 4 + r, count)] = level[r].astype(jnp.float32)
    turn(stack, flat, 0)
    flat[lon:, :] = jnp.zeros((flat.shape[0] - lon, LANES), jnp.float32)
    place = lax.broadcasted_iota(jnp.int32, (size, LANES), 1) // BLOCK
    first = lax.rem(place - mine + count, count) < count // 2
    for c in range(count):
        at = c * chunk
        target_ref[slot(c)] = jnp.where(
            first, flat[at : at + size, :], flat[at + half : at + half + size, :]
        )


def spread(tiles):
    count = len(tiles)
    lane = lax.broadcasted_iota(jnp.int32, tiles[0].shape, 1) // BLOCK
    tiles = [tiles[(count - t) % count] for t in range(count)]
    bit = 1
    while bit < count:
        upper = (lane & bit) != 0
        tiles = [jnp.where(upper, tiles[t - bit], tiles[t]) for t in range(count)]
        bit *= 2
    return tiles


def gathered(tiles):
    return [
        z if t == 0 else pltpu.roll(z, LANES - BLOCK * t, 1) for t, z in enumerate(spread(tiles))
    ]


def scattered(tiles):
    return spread([x if t == 0 else pltpu.roll(x, BLOCK * t, 1) for t, x in enumerate(tiles)])


def times_exact(x, matrix, parts):
    total = None
    for part in range(parts):
        piece = x.astype(jnp.bfloat16)
        term = jnp.dot(piece, matrix, preferred_element_type=jnp.float32)
        total = term if total is None else total + term
        if part < parts - 1:
            x = x - piece.astype(jnp.float32)
    return total


def unpack_state(raw_ref, out_ref):
    count, width, _ = raw_ref.shape
    for i in range(width // BLOCK):
        at = pl.ds(i * BLOCK, BLOCK)
        for k, tile in enumerate(gathered([raw_ref[s, at, :] for s in range(count)])):
            out_ref[k, at, :] = tile


def core_kernel(own_ref, near_ref, far_ref, place, out_ref, *scratch):
    buffers = (scratch[0:4], scratch[4:8])
    geo, spin, result = scratch[8:11]
    count, width, _ = own_ref.shape
    chunk = out_ref.shape[1]
    rim = (width - chunk) // 2
    lat = lax.axis_index("lat")
    lat_rows = lax.axis_size("lat") * 4
    rows = 12

    odd = lax.rem(lat, 2)
    for ref, base in ((far_ref, 8 * odd), (own_ref, 4), (near_ref, 8 - 8 * odd)):
        for f in range(4):
            buffers[0][f][pl.ds(base, 4)] = ref[4 * f : 4 * f + 4]

    def get(step, f, j):
        return buffers[step % 2][f][j]

    row_level = lax.broadcasted_iota(jnp.int32, (LANES, LANES), 0)
    col_level = lax.broadcasted_iota(jnp.int32, (LANES, LANES), 1)
    below = jnp.where(row_level > col_level, 1.0, jnp.where(row_level == col_level, 0.5, 0.0))
    below = below.astype(jnp.bfloat16)
    above = jnp.where(row_level < col_level, 1.0, 0.0).astype(jnp.bfloat16)
    slope = 0.05 / math.sqrt(LANES)

    row_index = lax.broadcasted_iota(jnp.int32, (16, LANES), 0) + (lat * 4 - 4)
    angle = math.pi * ((row_index.astype(jnp.float32) + 0.5) / lat_rows - 0.5)
    spin[...] = 0.15 * jnp.sin(angle)

    def east(x):
        return pltpu.roll(x, width - 1, 0)

    def west(x):
        return pltpu.roll(x, 1, 0)

    def upwind(speed, behind, ahead):
        return speed * jnp.where(speed > 0.0, behind, ahead)

    for step in range(STEPS):
        new = buffers[1 - step % 2]
        size = rows - 2 * step
        span = range(step, rows - step)
        load = jnp.concatenate([get(step, 3, j) * get(step, 2, j) for j in span], axis=0)
        heights = slope * times_exact(load, below, 3)
        geo[step : rows - step] = heights.reshape(size, width, LANES)
        flux_down = None
        for j in span:
            v, t, d = (get(step, f, j) for f in (1, 2, 3))
            if j == rows - step - 1:
                break
            v_n, t_n, d_n = (get(step, f, j + 1) for f in (1, 2, 3))
            flux_up = upwind(v + v_n, d, d_n)
            if flux_down is not None:
                u, t_s, g = get(step, 0, j), get(step, 2, j - 1), geo[j]
                cor = spin[j : j + 1, :]
                flux_x = upwind(u + east(u), d, east(d))
                new[0][j] = u - (east(g) - west(g)) + cor * v
                new[1][j] = v - (geo[j + 1] - geo[j - 1]) - cor * u
                new[2][j] = t - 0.05 * (u * (east(t) - west(t)) + v * (t_n - t_s))
                new[3][j] = d - 0.05 * (flux_x - west(flux_x) + flux_up - flux_down)
            flux_down = flux_up

        if step + 1 < 4:

            @pl.when(lat == 0)
            def _():
                for ref in new[1:]:
                    ref[:4] = jnp.zeros((4, width, LANES), jnp.float32)

            @pl.when(lat == lax.axis_size("lat") - 1)
            def _():
                for ref in new[1:]:
                    ref[8:] = jnp.zeros((4, width, LANES), jnp.float32)

    u, v, t, d = (ref[4:8, rim : rim + chunk, :] for ref in buffers[STEPS % 2])
    for f, q in enumerate((u * d, v * d, t * d, d)):
        result[4 * f : 4 * f + 4] = q
    flat = result[...].reshape(count * chunk, LANES)
    prefix = times_exact(flat, above, 3).reshape(count, chunk, LANES)
    lane = lax.broadcasted_iota(jnp.int32, (chunk, LANES), 1)
    for r in range(4):
        source = place[4 + r].astype(jnp.int32)
        part = place[r]
        for f in range(4):
            k = 4 * f + r
            mass = jnp.take_along_axis(prefix[k], source, axis=1) + part * jnp.take_along_axis(
                result[k], source, axis=1
            )
            result[k] = mass - jnp.where(lane == 0, 0.0, pltpu.roll(mass, 1, 1))
    for i in range(chunk // BLOCK):
        at = pl.ds(i * BLOCK, BLOCK)
        for s, tile in enumerate(scattered([result[k, at, :] for k in range(count)])):
            out_ref[s, at, :] = tile


def unpack_target(raw_ref, place):
    count, size, _ = raw_ref.shape
    half = place.shape[1] // 2
    for i in range(size // BLOCK):
        at = pl.ds(i * BLOCK, BLOCK)
        tiles = gathered([raw_ref[s, at, :] for s in range(count)])
        keep = min(BLOCK, half - i * BLOCK)
        for j in range(2):
            for k in range(8):
                start = j * half + i * BLOCK
                place[k, start : start + keep, :] = tiles[8 * j + k][:keep]


def receive_kernel(in_ref, *refs):
    outs, turned, flat = refs[:4], refs[4], refs[5]
    rows, _, lon = outs[0].shape
    count, chunk, _ = in_ref.shape
    mine = lax.axis_index("lev")
    for c in range(count):
        flat[c * chunk : (c + 1) * chunk, :] = in_ref[slot(c)]
    for at in range(0, lon, LANES):
        turned[:, :, at : at + LANES] = flat[at : at + LANES, :].T.reshape(count, BLOCK, LANES)
    for f, ref in enumerate(outs):
        for r in range(rows):
            ref[r] = turned[lax.rem(mine + rows * f + r, count)]


def call(kernel, ins, outs, scratch, *args, limit=24 * 2**20, flops=0, space=pltpu.VMEM):
    shapes = [jax.ShapeDtypeStruct(shape, jnp.float32) for shape in outs]
    moved = sum(4 * math.prod(a.shape) for a in (*args, *shapes))
    return pl.pallas_call(
        kernel,
        out_shape=shapes,
        in_specs=[pl.BlockSpec(memory_space=ins)] * len(args),
        out_specs=[pl.BlockSpec(memory_space=space)] * len(outs),
        scratch_shapes=[
            pltpu.VMEM(shape, jnp.float32) if isinstance(shape, tuple) else shape
            for shape in scratch
        ],
        cost_estimate=pl.CostEstimate(flops=flops, bytes_accessed=moved, transcendentals=0),
        compiler_params=pltpu.CompilerParams(vmem_limit_bytes=limit),
    )(*args)


def body(wind_east, wind_north, pot_temp, thickness, source_level, fraction):
    rows, depth, lon = wind_east.shape
    count = lax.axis_size("lev")
    blocks = lax.axis_size("lat")
    chunk = lon // count
    width = chunk + 2 * STEPS
    size = -(-(chunk // 2) // BLOCK) * BLOCK
    slab = wind_east.shape
    stack = (count, depth, lon)
    column = (count, chunk, LANES)
    (state,) = call(
        send_state, pltpu.HBM, [(count, width, LANES)],
        [stack, (lon + 2 * BLOCK, LANES)]
        + [pltpu.SemaphoreType.DMA((4 * rows,)), pltpu.SemaphoreType.DMA((count,))],
        wind_east, wind_north, pot_temp, thickness, limit=60 * 2**20, space=pltpu.HBM,
    )
    (target,) = call(
        send_target, pltpu.HBM, [(count, size, LANES)],
        [slab, pltpu.VMEM(slab, jnp.int32), stack, (lon + BLOCK, LANES)]
        + [pltpu.SemaphoreType.DMA((2,))],
        fraction, source_level, limit=60 * 2**20,
    )
    own = lax.all_to_all(state, "lev", 0, 0, tiled=True)
    own, target = lax.optimization_barrier((own, target))
    (own,) = call(unpack_state, pltpu.VMEM, [(count, width, LANES)], [], own)
    across = []
    for i in range(1, blocks - 1, 2):
        for k in range(count):
            m = k ^ 1 if i + 1 == blocks // 2 else k
            across += [(i * count + k, (i + 1) * count + m), ((i + 1) * count + m, i * count + k)]
    far = lax.ppermute(own, ("lat", "lev"), across)
    near = lax.ppermute(own, "lat", [(i, i ^ 1) for i in range(blocks)])
    target = lax.all_to_all(target, "lev", 0, 0, tiled=True)
    (place,) = call(unpack_target, pltpu.VMEM, [(8, chunk, LANES)], [], target, flops=2 * 10**10)
    (contents,) = call(
        core_kernel, pltpu.VMEM, [column],
        [(3 * rows, width, LANES)] * 9 + [(16, LANES), column],
        own, near, far, place, flops=3 * 10**8,
    )
    contents = lax.all_to_all(contents, "lev", 0, 0, tiled=True)
    return tuple(call(receive_kernel, pltpu.VMEM, [slab] * 4, [stack, (lon, LANES)], contents))


def solution(mesh):
    placed = P("lat", "lev", None)
    return jax.shard_map(
        body, mesh=mesh, in_specs=(placed,) * 6, out_specs=(placed,) * 4, check_vma=False
    )
```

time: 81.9 us -> 81.5 us (level)
  the two profiles are of different devices: /device:TPU:192 before, /device:TPU:449 now
where the time goes in v4:
time: 81.5 us; the launch traced here: 81 us
  blocking collectives  26.4 us (32%)
  waiting for transfers between devices  25.9 us (32%)
  starting transfers between devices  18.2 us (22%)
  Pallas kernels  9.81 us (12%)
    all_to_all x1, blocking collectives, body(): contents = lax.all_to_all(contents, 'lev', 0, 0, tiled=True)  26.4 us
    all_to_all x1, waiting for transfers between devices, body(): own = lax.all_to_all(state, 'lev', 0, 0, tiled=True)  16.1 us
    pallas_call x6, Pallas kernels, call(): pl.pallas_call(kernel, out_shape=shapes, in_specs=[pl.BlockSpec(memory_sp...  9.81 us
    all_to_all x1, starting transfers between devices, body(): own = lax.all_to_all(state, 'lev', 0, 0, tiled=True)  7.86 us
    all_to_all x1, waiting for transfers between devices, body(): target = lax.all_to_all(target, 'lev', 0, 0, tiled=True)  5.47 us
    all_to_all x1, starting transfers between devices, body(): target = lax.all_to_all(target, 'lev', 0, 0, tiled=True)  5.03 us
    ppermute x1, waiting for transfers between devices, body(): far = lax.ppermute(own, ('lat', 'lev'), across)  4.27 us
    ppermute x1, starting transfers between devices, body(): near = lax.ppermute(own, 'lat', [(i, i ^ 1) for i in range(blocks)])  3.38 us
  transfers between devices with their start and end apart: 4, of which 3 were waited for; matrix products, arithmetic and copies ran while one was open for 0% of the time, Pallas kernels for 3%

profile of v4, /device:TPU:449, one launch (start us, length us, event | category | flops | bytes accessed | tf_op | source)
XLA Modules:
  0.0 81.0 jit_solution(8316319462755226731)
XLA Ops:
  0.6 2.3 %shard_map.93 = f32[16,80,128]{2,1,0:T(8,128)} custom-call(f32[4,8,1152]{2,1,0:T(8,128)} %u_in.1, f32[4,8,1152]{2,1,0:T(8,128)} %v_in.1, f32[4,8,1152]{2,1,0:T(8,128)} %t_in.1, f32[4,8,1152]{2,1,0:T(8,128)} %d_in.1), custom_call_target="tpu_custom_call" | custom-call | bytes 1245184 | tf_op jit(solution)/shard_map/pallas_call | solution.py:262
  2.9 7.9 %all-to-all-start = ((f32[16,80,128]{2,1,0:T(8,128)}), f32[16,80,128]{2,1,0:T(8,128)S(1)}, u32[]{:S(2)}, u32[]{:S(2)}) async-start(f32[16,80,128]{2,1,0:T(8,128)} %shard_map.93), calls=%async_computation | async-start | bytes 1310720 | tf_op jit(solution)/shard_map/all_to_all | solution.py:298
  10.8 2.1 %shard_map.94 = f32[16,40,128]{2,1,0:T(8,128)} custom-call(f32[4,8,1152]{2,1,0:T(8,128)} %f_in.1, s32[4,8,1152]{2,1,0:T(8,128)} %s_in.1), custom_call_target="tpu_custom_call" | custom-call | bytes 622592 | tf_op jit(solution)/shard_map/pallas_call | solution.py:262
  12.9 16.1 %all-to-all-done.raw_ref = f32[16,80,128]{2,1,0:T(8,128)S(1)} async-done(((f32[16,80,128]{2,1,0:T(8,128)}), f32[16,80,128]{2,1,0:T(8,128)S(1)}, u32[]{:S(2)}, u32[]{:S(2)}) %all-to-all-start) | async-done | bytes 655392 | tf_op jit(solution)/shard_map/all_to_all | solution.py:298
  29.0 5.0 %all-to-all-start.1 = ((f32[16,40,128]{2,1,0:T(8,128)}), f32[16,40,128]{2,1,0:T(8,128)S(1)}, u32[]{:S(2)}, u32[]{:S(2)}) async-start(f32[16,40,128]{2,1,0:T(8,128)} %shard_map.94), calls=%async_computation.1 | async-start | bytes 655360 | tf_op jit(solution)/shard_map/all_to_all | solution.py:308
  34.1 0.2 shard_map.95.own_ref
  34.3 1.9 %collective-permute-start.1 = (f32[16,80,128]{2,1,0:T(8,128)S(1)}, f32[16,80,128]{2,1,0:T(8,128)S(1)}, u32[]{:S(2)}, u32[]{:S(2)}) collective-permute-start(f32[16,80,128]{2,1,0:T(8,128)S(1)} %shard_map.95.own_ref), channel_id=1, source_target_pairs={{16,32},{32,16},{17,33},{33,17},{18,34},{34,18},{19,35},{35,19},{2... | collective-permute-start | bytes 1966088 | tf_op jit(solution)/shard_map/ppermute | solution.py:306
  36.2 3.4 %collective-permute-start = (f32[16,80,128]{2,1,0:T(8,128)S(1)}, f32[16,80,128]{2,1,0:T(8,128)S(1)}, u32[]{:S(2)}, u32[]{:S(2)}) collective-permute-start(f32[16,80,128]{2,1,0:T(8,128)S(1)} %shard_map.95.own_ref), channel_id=1, source_target_pairs={{0,16},{16,0},{32,48},{48,32},{64,80},{80,64},{96,112},{112,96},{1... | collective-permute-start | bytes 1966088 | tf_op jit(solution)/shard_map/ppermute | solution.py:307
  39.6 5.5 %all-to-all-done.1.raw_ref = f32[16,40,128]{2,1,0:T(8,128)S(1)} async-done(((f32[16,40,128]{2,1,0:T(8,128)}), f32[16,40,128]{2,1,0:T(8,128)S(1)}, u32[]{:S(2)}, u32[]{:S(2)}) %all-to-all-start.1) | async-done | bytes 327712 | tf_op jit(solution)/shard_map/all_to_all | solution.py:308
  45.1 0.2 shard_map.96.place
  45.2 4.3 %collective-permute-done.1.far_ref = f32[16,80,128]{2,1,0:T(8,128)S(1)} collective-permute-done((f32[16,80,128]{2,1,0:T(8,128)S(1)}, f32[16,80,128]{2,1,0:T(8,128)S(1)}, u32[]{:S(2)}, u32[]{:S(2)}) %collective-permute-start.1) | collective-permute-done | bytes 655392 | tf_op jit(solution)/shard_map/ppermute | solution.py:306
  49.5 0.0 collective-permute-done.near_ref
  49.5 4.0 %shard_map.97 = f32[16,72,128]{2,1,0:T(8,128)S(1)} custom-call(f32[16,80,128]{2,1,0:T(8,128)S(1)} %shard_map.95.own_ref, f32[16,80,128]{2,1,0:T(8,128)S(1)} %collective-permute-done.near_ref, f32[16,80,128]{2,1,0:T(8,128)S(1)} %collective-permute-done.1.far_ref, f32[8,72,128]{2,1,0:T(8,128)S(1)} %shard_map.96.place), custom_call_target="tpu_custom_call" | custom-call | flops 300000000 | bytes 2850816 | tf_op jit(solution)/shard_map/pallas_call | solution.py:262
  53.5 26.4 %all_to_all.15.in_ref = f32[16,72,128]{2,1,0:T(8,128)S(1)} all-to-all(f32[16,72,128]{2,1,0:T(8,128)S(1)} %shard_map.97), channel_id=1, replica_groups=mesh['lat'=32,'lev'=16] {'lev'}, dimensions={0} | all-to-all | bytes 1179648 | tf_op jit(solution)/shard_map/all_to_all | solution.py:315
  80.0 1.1 %shard_map.98 = (f32[4,8,1152]{2,1,0:T(8,128)}, f32[4,8,1152]{2,1,0:T(8,128)}, f32[4,8,1152]{2,1,0:T(8,128)}, f32[4,8,1152]{2,1,0:T(8,128)}) custom-call(f32[16,72,128]{2,1,0:T(8,128)S(1)} %all_to_all.15.in_ref), custom_call_target="tpu_custom_call" | custom-call | bytes 1179648 | tf_op jit(solution)/shard_map/pallas_call | solution.py:262
Async XLA Ops:
  2.9 26.1 %all-to-all-start = ((f32[16,80,128]{2,1,0:T(8,128)}), f32[16,80,128]{2,1,0:T(8,128)S(1)}, u32[]{:S(2)}, u32[]{:S(2)}) async-start(f32[16,80,128]{2,1,0:T(8,128)} %shard_map.93), calls=%async_computation | async-start | bytes 1310720 | tf_op jit(solution)/shard_map/all_to_all | solution.py:298
  29.0 16.1 %all-to-all-start.1 = ((f32[16,40,128]{2,1,0:T(8,128)}), f32[16,40,128]{2,1,0:T(8,128)S(1)}, u32[]{:S(2)}, u32[]{:S(2)}) async-start(f32[16,40,128]{2,1,0:T(8,128)} %shard_map.94), calls=%async_computation.1 | async-start | bytes 655360 | tf_op jit(solution)/shard_map/all_to_all | solution.py:308
  34.3 15.2 %collective-permute-start.1 = (f32[16,80,128]{2,1,0:T(8,128)S(1)}, f32[16,80,128]{2,1,0:T(8,128)S(1)}, u32[]{:S(2)}, u32[]{:S(2)}) collective-permute-start(f32[16,80,128]{2,1,0:T(8,128)S(1)} %shard_map.95.own_ref), channel_id=1, source_target_pairs={{16,32},{32,16},{17,33},{33,17},{18,34},{34,18},{19,35},{35,19},{2... | collective-permute-start | bytes 1966088 | tf_op jit(solution)/shard_map/ppermute | solution.py:306
  36.2 13.3 %collective-permute-start = (f32[16,80,128]{2,1,0:T(8,128)S(1)}, f32[16,80,128]{2,1,0:T(8,128)S(1)}, u32[]{:S(2)}, u32[]{:S(2)}) collective-permute-start(f32[16,80,128]{2,1,0:T(8,128)S(1)} %shard_map.95.own_ref), channel_id=1, source_target_pairs={{0,16},{16,0},{32,48},{48,32},{64,80},{80,64},{96,112},{112,96},{1... | collective-permute-start | bytes 1966088 | tf_op jit(solution)/shard_map/ppermute | solution.py:307

commit v5 on v4

--- a/solution.py
+++ b/solution.py
@@ -10,11 +10,18 @@
 STEPS = 4
 LANES = 128
 BLOCK = 8
+ORDER = [0, 1, 7, 6, 12, 13, 3, 2, 8, 9, 15, 14, 4, 5, 11, 10]
+RANK = [ORDER.index(i) for i in range(len(ORDER))]
+
+
+def exchange(x):
+    return lax.all_to_all(x, "lev", 0, 0, tiled=True, axis_index_groups=[ORDER])
 
 
 def slot(chunk):
     half = lax.axis_size("lat") // 2
-    return chunk + lax.div(lax.axis_index("lat"), half) * (1 - 2 * (chunk % 2))
+    swapped = lax.div(lax.axis_index("lat"), half)
+    return RANK[chunk] + swapped * (RANK[chunk ^ 1] - RANK[chunk])
 
 
 def fetch(sources, targets, sems):
@@ -126,12 +133,18 @@
     return total
 
 
-def unpack_state(raw_ref, out_ref):
+def unpack_state(raw_ref, out_ref, far_ref):
     count, width, _ = raw_ref.shape
+    odd = lax.rem(lax.axis_index("lat"), 2)
     for i in range(width // BLOCK):
         at = pl.ds(i * BLOCK, BLOCK)
-        for k, tile in enumerate(gathered([raw_ref[s, at, :] for s in range(count)])):
+        tiles = gathered([raw_ref[RANK[s], at, :] for s in range(count)])
+        for k, tile in enumerate(tiles):
             out_ref[k, at, :] = tile
+            if k < 3:
+                tile = jnp.where(odd == 1, tiles[k + 1], tile)
+            if k != 3:
+                far_ref[k - (k > 3), at, :] = tile
 
 
 def core_kernel(own_ref, near_ref, far_ref, place, out_ref, *scratch):
@@ -145,11 +158,15 @@
     rows = 12
 
     odd = lax.rem(lat, 2)
-    for ref, base in ((far_ref, 8 * odd), (own_ref, 4), (near_ref, 8 - 8 * odd)):
-        for f in range(4):
-            buffers[0][f][pl.ds(base, 4)] = ref[4 * f : 4 * f + 4]
+    for f in range(4):
+        buffers[0][f][pl.ds(8 - 8 * odd, 4)] = near_ref[4 * f : 4 * f + 4]
+        if f > 0:
+            buffers[0][f][pl.ds(8 * odd, 4)] = far_ref[4 * f - 1 : 4 * f + 3]
+    buffers[0][0][pl.ds(1 + 7 * odd, 3)] = far_ref[:3]
 
     def get(step, f, j):
+        if step == 0 and 4 <= j < 8:
+            return own_ref[4 * f + j - 4]
         return buffers[step % 2][f][j]
 
     row_level = lax.broadcasted_iota(jnp.int32, (LANES, LANES), 0)
@@ -213,20 +230,21 @@
         result[4 * f : 4 * f + 4] = q
     flat = result[...].reshape(count * chunk, LANES)
     prefix = times_exact(flat, above, 3).reshape(count, chunk, LANES)
-    lane = lax.broadcasted_iota(jnp.int32, (chunk, LANES), 1)
-    for r in range(4):
-        source = place[4 + r].astype(jnp.int32)
-        part = place[r]
-        for f in range(4):
-            k = 4 * f + r
-            mass = jnp.take_along_axis(prefix[k], source, axis=1) + part * jnp.take_along_axis(
-                result[k], source, axis=1
-            )
-            result[k] = mass - jnp.where(lane == 0, 0.0, pltpu.roll(mass, 1, 1))
+    lane = lax.broadcasted_iota(jnp.int32, (BLOCK, LANES), 1)
     for i in range(chunk // BLOCK):
-        at = pl.ds(i * BLOCK, BLOCK)
-        for s, tile in enumerate(scattered([result[k, at, :] for k in range(count)])):
-            out_ref[s, at, :] = tile
+        at = slice(i * BLOCK, (i + 1) * BLOCK)
+        tiles = [None] * count
+        for r in range(4):
+            source = place[4 + r, at, :].astype(jnp.int32)
+            part = place[r, at, :]
+            ks = range(r, count, 4)
+            both = jnp.concatenate([prefix[k, at] for k in ks] + [result[k, at, :] for k in ks], axis=0)
+            picked = jnp.take_along_axis(both, jnp.concatenate([source] * 8, axis=0), axis=1)
+            for n, k in enumerate(ks):
+                mass = picked[8 * n : 8 * n + 8] + part * picked[32 + 8 * n : 40 + 8 * n]
+                tiles[k] = mass - jnp.where(lane == 0, 0.0, pltpu.roll(mass, 1, 1))
+        for s, tile in enumerate(scattered(tiles)):
+            out_ref[RANK[s], at, :] = tile
 
 
 def unpack_target(raw_ref, place):
@@ -234,7 +252,7 @@
     half = place.shape[1] // 2
     for i in range(size // BLOCK):
         at = pl.ds(i * BLOCK, BLOCK)
-        tiles = gathered([raw_ref[s, at, :] for s in range(count)])
+        tiles = gathered([raw_ref[RANK[s], at, :] for s in range(count)])
         keep = min(BLOCK, half - i * BLOCK)
         for j in range(2):
             for k in range(8):
@@ -295,24 +313,25 @@
         + [pltpu.SemaphoreType.DMA((2,))],
         fraction, source_level, limit=60 * 2**20,
     )
-    own = lax.all_to_all(state, "lev", 0, 0, tiled=True)
+    own = exchange(state)
     own, target = lax.optimization_barrier((own, target))
-    (own,) = call(unpack_state, pltpu.VMEM, [(count, width, LANES)], [], own)
+    block = (count, width, LANES)
+    own, edge = call(unpack_state, pltpu.VMEM, [block, (count - 1, *block[1:])], [], own)
     across = []
     for i in range(1, blocks - 1, 2):
         for k in range(count):
             m = k ^ 1 if i + 1 == blocks // 2 else k
             across += [(i * count + k, (i + 1) * count + m), ((i + 1) * count + m, i * count + k)]
-    far = lax.ppermute(own, ("lat", "lev"), across)
+    far = lax.ppermute(edge, ("lat", "lev"), across)
     near = lax.ppermute(own, "lat", [(i, i ^ 1) for i in range(blocks)])
-    target = lax.all_to_all(target, "lev", 0, 0, tiled=True)
+    target = exchange(target)
     (place,) = call(unpack_target, pltpu.VMEM, [(8, chunk, LANES)], [], target, flops=2 * 10**10)
     (contents,) = call(
         core_kernel, pltpu.VMEM, [column],
         [(3 * rows, width, LANES)] * 9 + [(16, LANES), column],
         own, near, far, place, flops=3 * 10**8,
     )
-    contents = lax.all_to_all(contents, "lev", 0, 0, tiled=True)
+    contents = exchange(contents)
     return tuple(call(receive_kernel, pltpu.VMEM, [slab] * 4, [stack, (lon, LANES)], contents))
 
 

time: 81.5 us -> 80.2 us (0.984)
  the two profiles are of different devices: /device:TPU:449 before, /device:TPU:193 now
where the time goes in v5:
time: 80.2 us; the launch traced here: 79.7 us
  blocking collectives  26.5 us (33%)
  starting transfers between devices  23.3 us (29%)
  waiting for transfers between devices  19.4 us (24%)
  Pallas kernels  9.79 us (12%)
    all_to_all x1, blocking collectives, exchange(): return lax.all_to_all(x, 'lev', 0, 0, tiled=True, axis_index_groups=[ORDER])  26.5 us
    all_to_all x2, starting transfers between devices, exchange(): return lax.all_to_all(x, 'lev', 0, 0, tiled=True, axis_index_groups=[ORDER])  14.3 us
    all_to_all x2, waiting for transfers between devices, exchange(): return lax.all_to_all(x, 'lev', 0, 0, tiled=True, axis_index_groups=[ORDER])  13.7 us
    pallas_call x6, Pallas kernels, call(): pl.pallas_call(kernel, out_shape=shapes, in_specs=[pl.BlockSpec(memory_sp...  9.79 us
    ppermute x1, starting transfers between devices, body(): far = lax.ppermute(edge, ('lat', 'lev'), across)  7.07 us
    ppermute x1, waiting for transfers between devices, body(): far = lax.ppermute(edge, ('lat', 'lev'), across)  5.63 us
    ppermute x1, starting transfers between devices, body(): near = lax.ppermute(own, 'lat', [(i, i ^ 1) for i in range(blocks)])  1.92 us
  transfers between devices with their start and end apart: 4, of which 3 were waited for; matrix products, arithmetic and copies ran while one was open for 0% of the time, Pallas kernels for 3%

profile of v5, /device:TPU:193, one launch (start us, length us, event | category | flops | bytes accessed | tf_op | source)
XLA Modules:
  0.0 79.7 jit_solution(15215184069163527751)
XLA Ops:
  0.6 2.3 %shard_map.93 = f32[16,80,128]{2,1,0:T(8,128)} custom-call(f32[4,8,1152]{2,1,0:T(8,128)} %u_in.1, f32[4,8,1152]{2,1,0:T(8,128)} %v_in.1, f32[4,8,1152]{2,1,0:T(8,128)} %t_in.1, f32[4,8,1152]{2,1,0:T(8,128)} %d_in.1), custom_call_target="tpu_custom_call" | custom-call | bytes 1245184 | tf_op jit(solution)/shard_map/pallas_call | solution.py:280
  2.9 7.9 %all-to-all-start = ((f32[16,80,128]{2,1,0:T(8,128)}), f32[16,80,128]{2,1,0:T(8,128)S(1)}, u32[]{:S(2)}, u32[]{:S(2)}) async-start(f32[16,80,128]{2,1,0:T(8,128)} %shard_map.93), calls=%async_computation | async-start | bytes 1310720 | tf_op jit(solution)/shard_map/all_to_all | solution.py:18
  10.8 2.1 %shard_map.94 = f32[16,40,128]{2,1,0:T(8,128)} custom-call(f32[4,8,1152]{2,1,0:T(8,128)} %f_in.1, s32[4,8,1152]{2,1,0:T(8,128)} %s_in.1), custom_call_target="tpu_custom_call" | custom-call | bytes 622592 | tf_op jit(solution)/shard_map/pallas_call | solution.py:280
  12.9 13.6 %all-to-all-done.raw_ref = f32[16,80,128]{2,1,0:T(8,128)S(1)} async-done(((f32[16,80,128]{2,1,0:T(8,128)}), f32[16,80,128]{2,1,0:T(8,128)S(1)}, u32[]{:S(2)}, u32[]{:S(2)}) %all-to-all-start) | async-done | bytes 655392 | tf_op jit(solution)/shard_map/all_to_all | solution.py:18
  26.5 6.5 %all-to-all-start.1 = ((f32[16,40,128]{2,1,0:T(8,128)}), f32[16,40,128]{2,1,0:T(8,128)S(1)}, u32[]{:S(2)}, u32[]{:S(2)}) async-start(f32[16,40,128]{2,1,0:T(8,128)} %shard_map.94), calls=%async_computation.1 | async-start | bytes 655360 | tf_op jit(solution)/shard_map/all_to_all | solution.py:18
  33.0 0.2 shard_map.95
  33.2 7.1 %collective-permute-start.1 = (f32[15,80,128]{2,1,0:T(8,128)S(1)}, f32[15,80,128]{2,1,0:T(8,128)S(1)}, u32[]{:S(2)}, u32[]{:S(2)}) collective-permute-start(f32[15,80,128]{2,1,0:T(8,128)S(1)} %get-tuple-element.10), channel_id=1, source_target_pairs={{16,32},{32,16},{17,33},{33,17},{18,34},{34,18},{19,35},{35,19},{2... | collective-permute-start | bytes 1843208 | tf_op jit(solution)/shard_map/ppermute | solution.py:325
  40.3 1.9 %collective-permute-start = (f32[16,80,128]{2,1,0:T(8,128)S(1)}, f32[16,80,128]{2,1,0:T(8,128)S(1)}, u32[]{:S(2)}, u32[]{:S(2)}) collective-permute-start(f32[16,80,128]{2,1,0:T(8,128)S(1)} %get-tuple-element.9.own_ref), channel_id=1, source_target_pairs={{0,16},{16,0},{32,48},{48,32},{64,80},{80,64},{96,112},{112,96},{1... | collective-permute-start | bytes 1966088 | tf_op jit(solution)/shard_map/ppermute | solution.py:326
  42.2 0.1 all-to-all-done.1.raw_ref
  42.3 0.2 shard_map.96.place
  42.5 5.6 %collective-permute-done.1.far_ref = f32[15,80,128]{2,1,0:T(8,128)S(1)} collective-permute-done((f32[15,80,128]{2,1,0:T(8,128)S(1)}, f32[15,80,128]{2,1,0:T(8,128)S(1)}, u32[]{:S(2)}, u32[]{:S(2)}) %collective-permute-start.1) | collective-permute-done | bytes 614432 | tf_op jit(solution)/shard_map/ppermute | solution.py:325
  48.1 0.0 collective-permute-done.near_ref
  48.1 4.0 %shard_map.97 = f32[16,72,128]{2,1,0:T(8,128)S(1)} custom-call(f32[16,80,128]{2,1,0:T(8,128)S(1)} %get-tuple-element.9.own_ref, f32[16,80,128]{2,1,0:T(8,128)S(1)} %collective-permute-done.near_ref, f32[15,80,128]{2,1,0:T(8,128)S(1)} %collective-permute-done.1.far_ref, f32[8,72,128]{2,1,0:T(8,128)S(1)} %shard_map.96.place), custom_call_target="tpu_custom_call" | custom-call | flops 300000000 | bytes 2809856 | tf_op jit(solution)/shard_map/pallas_call | solution.py:280
  52.1 26.5 %all_to_all.15.in_ref = f32[16,72,128]{2,1,0:T(8,128)S(1)} all-to-all(f32[16,72,128]{2,1,0:T(8,128)S(1)} %shard_map.97), channel_id=1, replica_groups={{0,1,7,6,12,13,3,2,8,9,15,14,4,5,11,10},{16,17,23,22,28,29,19,18,24,25,..., dimensions={0} | all-to-all | bytes 1179648 | tf_op jit(solution)/shard_map/all_to_all | solution.py:18
  78.7 1.1 %shard_map.98 = (f32[4,8,1152]{2,1,0:T(8,128)}, f32[4,8,1152]{2,1,0:T(8,128)}, f32[4,8,1152]{2,1,0:T(8,128)}, f32[4,8,1152]{2,1,0:T(8,128)}) custom-call(f32[16,72,128]{2,1,0:T(8,128)S(1)} %all_to_all.15.in_ref), custom_call_target="tpu_custom_call" | custom-call | bytes 1179648 | tf_op jit(solution)/shard_map/pallas_call | solution.py:280
Async XLA Ops:
  2.9 23.6 %all-to-all-start = ((f32[16,80,128]{2,1,0:T(8,128)}), f32[16,80,128]{2,1,0:T(8,128)S(1)}, u32[]{:S(2)}, u32[]{:S(2)}) async-start(f32[16,80,128]{2,1,0:T(8,128)} %shard_map.93), calls=%async_computation | async-start | bytes 1310720 | tf_op jit(solution)/shard_map/all_to_all | solution.py:18
  26.5 15.8 %all-to-all-start.1 = ((f32[16,40,128]{2,1,0:T(8,128)}), f32[16,40,128]{2,1,0:T(8,128)S(1)}, u32[]{:S(2)}, u32[]{:S(2)}) async-start(f32[16,40,128]{2,1,0:T(8,128)} %shard_map.94), calls=%async_computation.1 | async-start | bytes 655360 | tf_op jit(solution)/shard_map/all_to_all | solution.py:18
  33.2 14.9 %collective-permute-start.1 = (f32[15,80,128]{2,1,0:T(8,128)S(1)}, f32[15,80,128]{2,1,0:T(8,128)S(1)}, u32[]{:S(2)}, u32[]{:S(2)}) collective-permute-start(f32[15,80,128]{2,1,0:T(8,128)S(1)} %get-tuple-element.10), channel_id=1, source_target_pairs={{16,32},{32,16},{17,33},{33,17},{18,34},{34,18},{19,35},{35,19},{2... | collective-permute-start | bytes 1843208 | tf_op jit(solution)/shard_map/ppermute | solution.py:325
  40.3 7.8 %collective-permute-start = (f32[16,80,128]{2,1,0:T(8,128)S(1)}, f32[16,80,128]{2,1,0:T(8,128)S(1)}, u32[]{:S(2)}, u32[]{:S(2)}) collective-permute-start(f32[16,80,128]{2,1,0:T(8,128)S(1)} %get-tuple-element.9.own_ref), channel_id=1, source_target_pairs={{0,16},{16,0},{32,48},{48,32},{64,80},{80,64},{96,112},{112,96},{1... | collective-permute-start | bytes 1966088 | tf_op jit(solution)/shard_map/ppermute | solution.py:326

commit v6 on v5

--- a/solution.py
+++ b/solution.py
@@ -10,7 +10,7 @@
 STEPS = 4
 LANES = 128
 BLOCK = 8
-ORDER = [0, 1, 7, 6, 12, 13, 3, 2, 8, 9, 15, 14, 4, 5, 11, 10]
+ORDER = [8, 9, 15, 14, 4, 5, 11, 10, 0, 1, 7, 6, 12, 13, 3, 2]
 RANK = [ORDER.index(i) for i in range(len(ORDER))]
 
 

time: 80.2 us -> 76.8 us (0.958)
  the two profiles are of different devices: /device:TPU:193 before, /device:TPU:449 now
where the time goes in v6:
time: 76.8 us; the launch traced here: 75.9 us
  starting transfers between devices  22.2 us (29%)
  waiting for transfers between devices  21.8 us (28%)
  blocking collectives  21.4 us (28%)
  Pallas kernels  9.79 us (13%)
    all_to_all x1, blocking collectives, exchange(): return lax.all_to_all(x, 'lev', 0, 0, tiled=True, axis_index_groups=[ORDER])  21.4 us
    all_to_all x2, starting transfers between devices, exchange(): return lax.all_to_all(x, 'lev', 0, 0, tiled=True, axis_index_groups=[ORDER])  16.4 us
    all_to_all x2, waiting for transfers between devices, exchange(): return lax.all_to_all(x, 'lev', 0, 0, tiled=True, axis_index_groups=[ORDER])  14.5 us
    pallas_call x6, Pallas kernels, call(): pl.pallas_call(kernel, out_shape=shapes, in_specs=[pl.BlockSpec(memory_sp...  9.79 us
    ppermute x1, waiting for transfers between devices, body(): far = lax.ppermute(edge, ('lat', 'lev'), across)  7.25 us
    ppermute x1, starting transfers between devices, body(): near = lax.ppermute(own, 'lat', [(i, i ^ 1) for i in range(blocks)])  3.8 us
    ppermute x1, starting transfers between devices, body(): far = lax.ppermute(edge, ('lat', 'lev'), across)  1.92 us
  transfers between devices with their start and end apart: 4, of which 3 were waited for; matrix products, arithmetic and copies ran while one was open for 0% of the time, Pallas kernels for 3%

profile of v6, /device:TPU:449, one launch (start us, length us, event | category | flops | bytes accessed | tf_op | source)
XLA Modules:
  0.0 75.9 jit_solution(12235541776870071594)
XLA Ops:
  0.6 2.3 %shard_map.93 = f32[16,80,128]{2,1,0:T(8,128)} custom-call(f32[4,8,1152]{2,1,0:T(8,128)} %u_in.1, f32[4,8,1152]{2,1,0:T(8,128)} %v_in.1, f32[4,8,1152]{2,1,0:T(8,128)} %t_in.1, f32[4,8,1152]{2,1,0:T(8,128)} %d_in.1), custom_call_target="tpu_custom_call" | custom-call | bytes 1245184 | tf_op jit(solution)/shard_map/pallas_call | solution.py:280
  2.9 9.0 %all-to-all-start = ((f32[16,80,128]{2,1,0:T(8,128)}), f32[16,80,128]{2,1,0:T(8,128)S(1)}, u32[]{:S(2)}, u32[]{:S(2)}) async-start(f32[16,80,128]{2,1,0:T(8,128)} %shard_map.93), calls=%async_computation | async-start | bytes 1310720 | tf_op jit(solution)/shard_map/all_to_all | solution.py:18
  11.9 2.1 %shard_map.94 = f32[16,40,128]{2,1,0:T(8,128)} custom-call(f32[4,8,1152]{2,1,0:T(8,128)} %f_in.1, s32[4,8,1152]{2,1,0:T(8,128)} %s_in.1), custom_call_target="tpu_custom_call" | custom-call | bytes 622592 | tf_op jit(solution)/shard_map/pallas_call | solution.py:280
  14.0 12.9 %all-to-all-done.raw_ref = f32[16,80,128]{2,1,0:T(8,128)S(1)} async-done(((f32[16,80,128]{2,1,0:T(8,128)}), f32[16,80,128]{2,1,0:T(8,128)S(1)}, u32[]{:S(2)}, u32[]{:S(2)}) %all-to-all-start) | async-done | bytes 655392 | tf_op jit(solution)/shard_map/all_to_all | solution.py:18
  26.9 7.5 %all-to-all-start.1 = ((f32[16,40,128]{2,1,0:T(8,128)}), f32[16,40,128]{2,1,0:T(8,128)S(1)}, u32[]{:S(2)}, u32[]{:S(2)}) async-start(f32[16,40,128]{2,1,0:T(8,128)} %shard_map.94), calls=%async_computation.1 | async-start | bytes 655360 | tf_op jit(solution)/shard_map/all_to_all | solution.py:18
  34.4 0.2 shard_map.95
  34.6 1.9 %collective-permute-start.1 = (f32[15,80,128]{2,1,0:T(8,128)S(1)}, f32[15,80,128]{2,1,0:T(8,128)S(1)}, u32[]{:S(2)}, u32[]{:S(2)}) collective-permute-start(f32[15,80,128]{2,1,0:T(8,128)S(1)} %get-tuple-element.10), channel_id=1, source_target_pairs={{16,32},{32,16},{17,33},{33,17},{18,34},{34,18},{19,35},{35,19},{2... | collective-permute-start | bytes 1843208 | tf_op jit(solution)/shard_map/ppermute | solution.py:325
  36.5 3.8 %collective-permute-start = (f32[16,80,128]{2,1,0:T(8,128)S(1)}, f32[16,80,128]{2,1,0:T(8,128)S(1)}, u32[]{:S(2)}, u32[]{:S(2)}) collective-permute-start(f32[16,80,128]{2,1,0:T(8,128)S(1)} %get-tuple-element.9.own_ref), channel_id=1, source_target_pairs={{0,16},{16,0},{32,48},{48,32},{64,80},{80,64},{96,112},{112,96},{1... | collective-permute-start | bytes 1966088 | tf_op jit(solution)/shard_map/ppermute | solution.py:326
  40.3 1.6 %all-to-all-done.1.raw_ref = f32[16,40,128]{2,1,0:T(8,128)S(1)} async-done(((f32[16,40,128]{2,1,0:T(8,128)}), f32[16,40,128]{2,1,0:T(8,128)S(1)}, u32[]{:S(2)}, u32[]{:S(2)}) %all-to-all-start.1) | async-done | bytes 327712 | tf_op jit(solution)/shard_map/all_to_all | solution.py:18
  42.0 0.2 shard_map.96.place
  42.1 7.3 %collective-permute-done.1.far_ref = f32[15,80,128]{2,1,0:T(8,128)S(1)} collective-permute-done((f32[15,80,128]{2,1,0:T(8,128)S(1)}, f32[15,80,128]{2,1,0:T(8,128)S(1)}, u32[]{:S(2)}, u32[]{:S(2)}) %collective-permute-start.1) | collective-permute-done | bytes 614432 | tf_op jit(solution)/shard_map/ppermute | solution.py:325
  49.4 0.0 collective-permute-done.near_ref
  49.4 4.0 %shard_map.97 = f32[16,72,128]{2,1,0:T(8,128)S(1)} custom-call(f32[16,80,128]{2,1,0:T(8,128)S(1)} %get-tuple-element.9.own_ref, f32[16,80,128]{2,1,0:T(8,128)S(1)} %collective-permute-done.near_ref, f32[15,80,128]{2,1,0:T(8,128)S(1)} %collective-permute-done.1.far_ref, f32[8,72,128]{2,1,0:T(8,128)S(1)} %shard_map.96.place), custom_call_target="tpu_custom_call" | custom-call | flops 300000000 | bytes 2809856 | tf_op jit(solution)/shard_map/pallas_call | solution.py:280
  53.4 21.4 %all_to_all.15.in_ref = f32[16,72,128]{2,1,0:T(8,128)S(1)} all-to-all(f32[16,72,128]{2,1,0:T(8,128)S(1)} %shard_map.97), channel_id=1, replica_groups={{8,9,15,14,4,5,11,10,0,1,7,6,12,13,3,2},{24,25,31,30,20,21,27,26,16,17,..., dimensions={0} | all-to-all | bytes 1179648 | tf_op jit(solution)/shard_map/all_to_all | solution.py:18
  74.8 1.1 %shard_map.98 = (f32[4,8,1152]{2,1,0:T(8,128)}, f32[4,8,1152]{2,1,0:T(8,128)}, f32[4,8,1152]{2,1,0:T(8,128)}, f32[4,8,1152]{2,1,0:T(8,128)}) custom-call(f32[16,72,128]{2,1,0:T(8,128)S(1)} %all_to_all.15.in_ref), custom_call_target="tpu_custom_call" | custom-call | bytes 1179648 | tf_op jit(solution)/shard_map/pallas_call | solution.py:280
Async XLA Ops:
  2.9 24.0 %all-to-all-start = ((f32[16,80,128]{2,1,0:T(8,128)}), f32[16,80,128]{2,1,0:T(8,128)S(1)}, u32[]{:S(2)}, u32[]{:S(2)}) async-start(f32[16,80,128]{2,1,0:T(8,128)} %shard_map.93), calls=%async_computation | async-start | bytes 1310720 | tf_op jit(solution)/shard_map/all_to_all | solution.py:18
  26.9 15.1 %all-to-all-start.1 = ((f32[16,40,128]{2,1,0:T(8,128)}), f32[16,40,128]{2,1,0:T(8,128)S(1)}, u32[]{:S(2)}, u32[]{:S(2)}) async-start(f32[16,40,128]{2,1,0:T(8,128)} %shard_map.94), calls=%async_computation.1 | async-start | bytes 655360 | tf_op jit(solution)/shard_map/all_to_all | solution.py:18
  34.6 14.8 %collective-permute-start.1 = (f32[15,80,128]{2,1,0:T(8,128)S(1)}, f32[15,80,128]{2,1,0:T(8,128)S(1)}, u32[]{:S(2)}, u32[]{:S(2)}) collective-permute-start(f32[15,80,128]{2,1,0:T(8,128)S(1)} %get-tuple-element.10), channel_id=1, source_target_pairs={{16,32},{32,16},{17,33},{33,17},{18,34},{34,18},{19,35},{35,19},{2... | collective-permute-start | bytes 1843208 | tf_op jit(solution)/shard_map/ppermute | solution.py:325
  36.5 12.9 %collective-permute-start = (f32[16,80,128]{2,1,0:T(8,128)S(1)}, f32[16,80,128]{2,1,0:T(8,128)S(1)}, u32[]{:S(2)}, u32[]{:S(2)}) collective-permute-start(f32[16,80,128]{2,1,0:T(8,128)S(1)} %get-tuple-element.9.own_ref), channel_id=1, source_target_pairs={{0,16},{16,0},{32,48},{48,32},{64,80},{80,64},{96,112},{112,96},{1... | collective-permute-start | bytes 1966088 | tf_op jit(solution)/shard_map/ppermute | solution.py:326

commit v7 on v6

--- a/solution.py
+++ b/solution.py
@@ -10,18 +10,24 @@
 STEPS = 4
 LANES = 128
 BLOCK = 8
-ORDER = [8, 9, 15, 14, 4, 5, 11, 10, 0, 1, 7, 6, 12, 13, 3, 2]
-RANK = [ORDER.index(i) for i in range(len(ORDER))]
-
-
-def exchange(x):
-    return lax.all_to_all(x, "lev", 0, 0, tiled=True, axis_index_groups=[ORDER])
-
-
-def slot(chunk):
+STATE_ORDER = [8, 9, 15, 14, 4, 5, 11, 10, 0, 1, 7, 6, 12, 13, 3, 2]
+TARGET_ORDER = [0, 1, 7, 6, 12, 13, 3, 2, 8, 9, 15, 14, 4, 5, 11, 10]
+RESULT_ORDER = [8, 9, 15, 14, 4, 5, 11, 10, 0, 1, 7, 6, 12, 13, 3, 2]
+
+
+def rank(order):
+    return [order.index(i) for i in range(len(order))]
+
+
+def exchange(x, order):
+    return lax.all_to_all(x, "lev", 0, 0, tiled=True, axis_index_groups=[order])
+
+
+def slot(chunk, order):
     half = lax.axis_size("lat") // 2
     swapped = lax.div(lax.axis_index("lat"), half)
-    return RANK[chunk] + swapped * (RANK[chunk ^ 1] - RANK[chunk])
+    places = rank(order)
+    return places[chunk] + swapped * (places[chunk ^ 1] - places[chunk])
 
 
 def fetch(sources, targets, sems):
@@ -56,7 +62,7 @@
     base = BLOCK + rim
     outs = [
         pltpu.make_async_copy(
-            flat.at[pl.ds(BLOCK + c * chunk, width)], state_out.at[slot(c)], out_sems.at[c]
+            flat.at[pl.ds(BLOCK + c * chunk, width)], state_out.at[slot(c, STATE_ORDER)], out_sems.at[c]
         )
         for c in range(count)
     ]
@@ -95,7 +101,7 @@
     first = lax.rem(place - mine + count, count) < count // 2
     for c in range(count):
         at = c * chunk
-        target_ref[slot(c)] = jnp.where(
+        target_ref[slot(c, TARGET_ORDER)] = jnp.where(
             first, flat[at : at + size, :], flat[at + half : at + half + size, :]
         )
 
@@ -138,7 +144,7 @@
     odd = lax.rem(lax.axis_index("lat"), 2)
     for i in range(width // BLOCK):
         at = pl.ds(i * BLOCK, BLOCK)
-        tiles = gathered([raw_ref[RANK[s], at, :] for s in range(count)])
+        tiles = gathered([raw_ref[s, at, :] for s in rank(STATE_ORDER)])
         for k, tile in enumerate(tiles):
             out_ref[k, at, :] = tile
             if k < 3:
@@ -244,7 +250,7 @@
                 mass = picked[8 * n : 8 * n + 8] + part * picked[32 + 8 * n : 40 + 8 * n]
                 tiles[k] = mass - jnp.where(lane == 0, 0.0, pltpu.roll(mass, 1, 1))
         for s, tile in enumerate(scattered(tiles)):
-            out_ref[RANK[s], at, :] = tile
+            out_ref[rank(RESULT_ORDER)[s], at, :] = tile
 
 
 def unpack_target(raw_ref, place):
@@ -252,7 +258,7 @@
     half = place.shape[1] // 2
     for i in range(size // BLOCK):
         at = pl.ds(i * BLOCK, BLOCK)
-        tiles = gathered([raw_ref[RANK[s], at, :] for s in range(count)])
+        tiles = gathered([raw_ref[s, at, :] for s in rank(TARGET_ORDER)])
         keep = min(BLOCK, half - i * BLOCK)
         for j in range(2):
             for k in range(8):
@@ -266,7 +272,7 @@
     count, chunk, _ = in_ref.shape
     mine = lax.axis_index("lev")
     for c in range(count):
-        flat[c * chunk : (c + 1) * chunk, :] = in_ref[slot(c)]
+        flat[c * chunk : (c + 1) * chunk, :] = in_ref[slot(c, RESULT_ORDER)]
     for at in range(0, lon, LANES):
         turned[:, :, at : at + LANES] = flat[at : at + LANES, :].T.reshape(count, BLOCK, LANES)
     for f, ref in enumerate(outs):
@@ -313,7 +319,7 @@
         + [pltpu.SemaphoreType.DMA((2,))],
         fraction, source_level, limit=60 * 2**20,
     )
-    own = exchange(state)
+    own = exchange(state, STATE_ORDER)
     own, target = lax.optimization_barrier((own, target))
     block = (count, width, LANES)
     own, edge = call(unpack_state, pltpu.VMEM, [block, (count - 1, *block[1:])], [], own)
@@ -324,14 +330,14 @@
             across += [(i * count + k, (i + 1) * count + m), ((i + 1) * count + m, i * count + k)]
     far = lax.ppermute(edge, ("lat", "lev"), across)
     near = lax.ppermute(own, "lat", [(i, i ^ 1) for i in range(blocks)])
-    target = exchange(target)
+    target = exchange(target, TARGET_ORDER)
     (place,) = call(unpack_target, pltpu.VMEM, [(8, chunk, LANES)], [], target, flops=2 * 10**10)
     (contents,) = call(
         core_kernel, pltpu.VMEM, [column],
         [(3 * rows, width, LANES)] * 9 + [(16, LANES), column],
         own, near, far, place, flops=3 * 10**8,
     )
-    contents = exchange(contents)
+    contents = exchange(contents, RESULT_ORDER)
     return tuple(call(receive_kernel, pltpu.VMEM, [slab] * 4, [stack, (lon, LANES)], contents))
 
 

time: 76.8 us -> 75.8 us (0.987)
  blocking collectives: 21.4 us -> 22.8 us
  starting transfers between devices: 22.2 us -> 20.8 us
    all_to_all x2, starting transfers between devices: 16.4 us -> 14.5 us  [exchange(): return lax.all_to_all(x, 'lev', 0, 0, tiled=True, axis_index_groups=[order])]
    ppermute x1, waiting for transfers between devices: 7.25 us -> 5.54 us  [body(): far = lax.ppermute(edge, ('lat', 'lev'), across)]
    all_to_all x1, blocking collectives: 21.4 us -> 22.8 us  [exchange(): return lax.all_to_all(x, 'lev', 0, 0, tiled=True, axis_index_groups=[order])]
    all_to_all x2, waiting for transfers between devices: 14.5 us -> 15.7 us  [exchange(): return lax.all_to_all(x, 'lev', 0, 0, tiled=True, axis_index_groups=[order])]
where the time goes in v7:
time: 75.8 us; the launch traced here: 75.3 us
  blocking collectives  22.8 us (30%)
  waiting for transfers between devices  21.3 us (28%)
  starting transfers between devices  20.8 us (27%)
  Pallas kernels  9.8 us (13%)
    all_to_all x1, blocking collectives, exchange(): return lax.all_to_all(x, 'lev', 0, 0, tiled=True, axis_index_groups=[order])  22.8 us
    all_to_all x2, waiting for transfers between devices, exchange(): return lax.all_to_all(x, 'lev', 0, 0, tiled=True, axis_index_groups=[order])  15.7 us
    all_to_all x2, starting transfers between devices, exchange(): return lax.all_to_all(x, 'lev', 0, 0, tiled=True, axis_index_groups=[order])  14.5 us
    pallas_call x6, Pallas kernels, call(): pl.pallas_call(kernel, out_shape=shapes, in_specs=[pl.BlockSpec(memory_sp...  9.8 us
    ppermute x1, waiting for transfers between devices, body(): far = lax.ppermute(edge, ('lat', 'lev'), across)  5.54 us
    ppermute x1, starting transfers between devices, body(): near = lax.ppermute(own, 'lat', [(i, i ^ 1) for i in range(blocks)])  4.34 us
    ppermute x1, starting transfers between devices, body(): far = lax.ppermute(edge, ('lat', 'lev'), across)  1.92 us
  transfers between devices with their start and end apart: 4, of which 3 were waited for; matrix products, arithmetic and copies ran while one was open for 0% of the time, Pallas kernels for 3%

profile of v7, /device:TPU:449, one launch (start us, length us, event | category | flops | bytes accessed | tf_op | source)
XLA Modules:
  0.0 75.3 jit_solution(7196332702373575830)
XLA Ops:
  0.6 2.3 %shard_map.93 = f32[16,80,128]{2,1,0:T(8,128)} custom-call(f32[4,8,1152]{2,1,0:T(8,128)} %u_in.1, f32[4,8,1152]{2,1,0:T(8,128)} %v_in.1, f32[4,8,1152]{2,1,0:T(8,128)} %t_in.1, f32[4,8,1152]{2,1,0:T(8,128)} %d_in.1), custom_call_target="tpu_custom_call" | custom-call | bytes 1245184 | tf_op jit(solution)/shard_map/pallas_call | solution.py:286
  2.9 9.0 %all-to-all-start = ((f32[16,80,128]{2,1,0:T(8,128)}), f32[16,80,128]{2,1,0:T(8,128)S(1)}, u32[]{:S(2)}, u32[]{:S(2)}) async-start(f32[16,80,128]{2,1,0:T(8,128)} %shard_map.93), calls=%async_computation | async-start | bytes 1310720 | tf_op jit(solution)/shard_map/all_to_all | solution.py:23
  11.9 2.1 %shard_map.94 = f32[16,40,128]{2,1,0:T(8,128)} custom-call(f32[4,8,1152]{2,1,0:T(8,128)} %f_in.1, s32[4,8,1152]{2,1,0:T(8,128)} %s_in.1), custom_call_target="tpu_custom_call" | custom-call | bytes 622592 | tf_op jit(solution)/shard_map/pallas_call | solution.py:286
  14.0 12.9 %all-to-all-done.raw_ref = f32[16,80,128]{2,1,0:T(8,128)S(1)} async-done(((f32[16,80,128]{2,1,0:T(8,128)}), f32[16,80,128]{2,1,0:T(8,128)S(1)}, u32[]{:S(2)}, u32[]{:S(2)}) %all-to-all-start) | async-done | bytes 655392 | tf_op jit(solution)/shard_map/all_to_all | solution.py:23
  26.9 5.5 %all-to-all-start.1 = ((f32[16,40,128]{2,1,0:T(8,128)}), f32[16,40,128]{2,1,0:T(8,128)S(1)}, u32[]{:S(2)}, u32[]{:S(2)}) async-start(f32[16,40,128]{2,1,0:T(8,128)} %shard_map.94), calls=%async_computation.1 | async-start | bytes 655360 | tf_op jit(solution)/shard_map/all_to_all | solution.py:23
  32.4 0.2 shard_map.95
  32.7 1.9 %collective-permute-start.1 = (f32[15,80,128]{2,1,0:T(8,128)S(1)}, f32[15,80,128]{2,1,0:T(8,128)S(1)}, u32[]{:S(2)}, u32[]{:S(2)}) collective-permute-start(f32[15,80,128]{2,1,0:T(8,128)S(1)} %get-tuple-element.10), channel_id=1, source_target_pairs={{16,32},{32,16},{17,33},{33,17},{18,34},{34,18},{19,35},{35,19},{2... | collective-permute-start | bytes 1843208 | tf_op jit(solution)/shard_map/ppermute | solution.py:331
  34.6 4.3 %collective-permute-start = (f32[16,80,128]{2,1,0:T(8,128)S(1)}, f32[16,80,128]{2,1,0:T(8,128)S(1)}, u32[]{:S(2)}, u32[]{:S(2)}) collective-permute-start(f32[16,80,128]{2,1,0:T(8,128)S(1)} %get-tuple-element.9.own_ref), channel_id=1, source_target_pairs={{0,16},{16,0},{32,48},{48,32},{64,80},{80,64},{96,112},{112,96},{1... | collective-permute-start | bytes 1966088 | tf_op jit(solution)/shard_map/ppermute | solution.py:332
  38.9 2.8 %all-to-all-done.1.raw_ref = f32[16,40,128]{2,1,0:T(8,128)S(1)} async-done(((f32[16,40,128]{2,1,0:T(8,128)}), f32[16,40,128]{2,1,0:T(8,128)S(1)}, u32[]{:S(2)}, u32[]{:S(2)}) %all-to-all-start.1) | async-done | bytes 327712 | tf_op jit(solution)/shard_map/all_to_all | solution.py:23
  41.8 0.2 shard_map.96.place
  41.9 5.5 %collective-permute-done.1.far_ref = f32[15,80,128]{2,1,0:T(8,128)S(1)} collective-permute-done((f32[15,80,128]{2,1,0:T(8,128)S(1)}, f32[15,80,128]{2,1,0:T(8,128)S(1)}, u32[]{:S(2)}, u32[]{:S(2)}) %collective-permute-start.1) | collective-permute-done | bytes 614432 | tf_op jit(solution)/shard_map/ppermute | solution.py:331
  47.5 0.0 collective-permute-done.near_ref
  47.5 4.0 %shard_map.97 = f32[16,72,128]{2,1,0:T(8,128)S(1)} custom-call(f32[16,80,128]{2,1,0:T(8,128)S(1)} %get-tuple-element.9.own_ref, f32[16,80,128]{2,1,0:T(8,128)S(1)} %collective-permute-done.near_ref, f32[15,80,128]{2,1,0:T(8,128)S(1)} %collective-permute-done.1.far_ref, f32[8,72,128]{2,1,0:T(8,128)S(1)} %shard_map.96.place), custom_call_target="tpu_custom_call" | custom-call | flops 300000000 | bytes 2809856 | tf_op jit(solution)/shard_map/pallas_call | solution.py:286
  51.5 22.8 %all_to_all.15.in_ref = f32[16,72,128]{2,1,0:T(8,128)S(1)} all-to-all(f32[16,72,128]{2,1,0:T(8,128)S(1)} %shard_map.97), channel_id=1, replica_groups={{8,9,15,14,4,5,11,10,0,1,7,6,12,13,3,2},{24,25,31,30,20,21,27,26,16,17,..., dimensions={0} | all-to-all | bytes 1179648 | tf_op jit(solution)/shard_map/all_to_all | solution.py:23
  74.3 1.1 %shard_map.98 = (f32[4,8,1152]{2,1,0:T(8,128)}, f32[4,8,1152]{2,1,0:T(8,128)}, f32[4,8,1152]{2,1,0:T(8,128)}, f32[4,8,1152]{2,1,0:T(8,128)}) custom-call(f32[16,72,128]{2,1,0:T(8,128)S(1)} %all_to_all.15.in_ref), custom_call_target="tpu_custom_call" | custom-call | bytes 1179648 | tf_op jit(solution)/shard_map/pallas_call | solution.py:286
Async XLA Ops:
  2.9 24.0 %all-to-all-start = ((f32[16,80,128]{2,1,0:T(8,128)}), f32[16,80,128]{2,1,0:T(8,128)S(1)}, u32[]{:S(2)}, u32[]{:S(2)}) async-start(f32[16,80,128]{2,1,0:T(8,128)} %shard_map.93), calls=%async_computation | async-start | bytes 1310720 | tf_op jit(solution)/shard_map/all_to_all | solution.py:23
  26.9 14.9 %all-to-all-start.1 = ((f32[16,40,128]{2,1,0:T(8,128)}), f32[16,40,128]{2,1,0:T(8,128)S(1)}, u32[]{:S(2)}, u32[]{:S(2)}) async-start(f32[16,40,128]{2,1,0:T(8,128)} %shard_map.94), calls=%async_computation.1 | async-start | bytes 655360 | tf_op jit(solution)/shard_map/all_to_all | solution.py:23
  32.7 14.8 %collective-permute-start.1 = (f32[15,80,128]{2,1,0:T(8,128)S(1)}, f32[15,80,128]{2,1,0:T(8,128)S(1)}, u32[]{:S(2)}, u32[]{:S(2)}) collective-permute-start(f32[15,80,128]{2,1,0:T(8,128)S(1)} %get-tuple-element.10), channel_id=1, source_target_pairs={{16,32},{32,16},{17,33},{33,17},{18,34},{34,18},{19,35},{35,19},{2... | collective-permute-start | bytes 1843208 | tf_op jit(solution)/shard_map/ppermute | solution.py:331
  34.6 12.9 %collective-permute-start = (f32[16,80,128]{2,1,0:T(8,128)S(1)}, f32[16,80,128]{2,1,0:T(8,128)S(1)}, u32[]{:S(2)}, u32[]{:S(2)}) collective-permute-start(f32[16,80,128]{2,1,0:T(8,128)S(1)} %get-tuple-element.9.own_ref), channel_id=1, source_target_pairs={{0,16},{16,0},{32,48},{48,32},{64,80},{80,64},{96,112},{112,96},{1... | collective-permute-start | bytes 1966088 | tf_op jit(solution)/shard_map/ppermute | solution.py:332

commit v8 on v7

--- a/solution.py
+++ b/solution.py
@@ -11,7 +11,7 @@
 LANES = 128
 BLOCK = 8
 STATE_ORDER = [8, 9, 15, 14, 4, 5, 11, 10, 0, 1, 7, 6, 12, 13, 3, 2]
-TARGET_ORDER = [0, 1, 7, 6, 12, 13, 3, 2, 8, 9, 15, 14, 4, 5, 11, 10]
+TARGET_ORDER = [0, 1, 9, 8, 4, 5, 13, 12, 2, 3, 11, 10, 6, 7, 15, 14]
 RESULT_ORDER = [8, 9, 15, 14, 4, 5, 11, 10, 0, 1, 7, 6, 12, 13, 3, 2]
 
 

time: 75.8 us -> 75.8 us (level)
  no operation moved by 1% of the time
where the time goes in v8:
time: 75.8 us; the launch traced here: 75.3 us
  blocking collectives  22.8 us (30%)
  waiting for transfers between devices  21.3 us (28%)
  starting transfers between devices  20.8 us (27%)
  Pallas kernels  9.8 us (13%)
    all_to_all x1, blocking collectives, exchange(): return lax.all_to_all(x, 'lev', 0, 0, tiled=True, axis_index_groups=[order])  22.8 us
    all_to_all x2, waiting for transfers between devices, exchange(): return lax.all_to_all(x, 'lev', 0, 0, tiled=True, axis_index_groups=[order])  16.4 us
    all_to_all x2, starting transfers between devices, exchange(): return lax.all_to_all(x, 'lev', 0, 0, tiled=True, axis_index_groups=[order])  14.5 us
    pallas_call x6, Pallas kernels, call(): pl.pallas_call(kernel, out_shape=shapes, in_specs=[pl.BlockSpec(memory_sp...  9.8 us
    ppermute x1, waiting for transfers between devices, body(): far = lax.ppermute(edge, ('lat', 'lev'), across)  4.88 us
    ppermute x1, starting transfers between devices, body(): near = lax.ppermute(own, 'lat', [(i, i ^ 1) for i in range(blocks)])  4.34 us
    ppermute x1, starting transfers between devices, body(): far = lax.ppermute(edge, ('lat', 'lev'), across)  1.92 us
  transfers between devices with their start and end apart: 4, of which 3 were waited for; matrix products, arithmetic and copies ran while one was open for 0% of the time, Pallas kernels for 3%

profile of v8, /device:TPU:449, one launch (start us, length us, event | category | flops | bytes accessed | tf_op | source)
XLA Modules:
  0.0 75.3 jit_solution(14149940543290691705)
XLA Ops:
  0.6 2.3 %shard_map.93 = f32[16,80,128]{2,1,0:T(8,128)} custom-call(f32[4,8,1152]{2,1,0:T(8,128)} %u_in.1, f32[4,8,1152]{2,1,0:T(8,128)} %v_in.1, f32[4,8,1152]{2,1,0:T(8,128)} %t_in.1, f32[4,8,1152]{2,1,0:T(8,128)} %d_in.1), custom_call_target="tpu_custom_call" | custom-call | bytes 1245184 | tf_op jit(solution)/shard_map/pallas_call | solution.py:286
  2.9 9.0 %all-to-all-start = ((f32[16,80,128]{2,1,0:T(8,128)}), f32[16,80,128]{2,1,0:T(8,128)S(1)}, u32[]{:S(2)}, u32[]{:S(2)}) async-start(f32[16,80,128]{2,1,0:T(8,128)} %shard_map.93), calls=%async_computation | async-start | bytes 1310720 | tf_op jit(solution)/shard_map/all_to_all | solution.py:23
  11.9 2.1 %shard_map.94 = f32[16,40,128]{2,1,0:T(8,128)} custom-call(f32[4,8,1152]{2,1,0:T(8,128)} %f_in.1, s32[4,8,1152]{2,1,0:T(8,128)} %s_in.1), custom_call_target="tpu_custom_call" | custom-call | bytes 622592 | tf_op jit(solution)/shard_map/pallas_call | solution.py:286
  14.0 12.9 %all-to-all-done.raw_ref = f32[16,80,128]{2,1,0:T(8,128)S(1)} async-done(((f32[16,80,128]{2,1,0:T(8,128)}), f32[16,80,128]{2,1,0:T(8,128)S(1)}, u32[]{:S(2)}, u32[]{:S(2)}) %all-to-all-start) | async-done | bytes 655392 | tf_op jit(solution)/shard_map/all_to_all | solution.py:23
  26.9 5.5 %all-to-all-start.1 = ((f32[16,40,128]{2,1,0:T(8,128)}), f32[16,40,128]{2,1,0:T(8,128)S(1)}, u32[]{:S(2)}, u32[]{:S(2)}) async-start(f32[16,40,128]{2,1,0:T(8,128)} %shard_map.94), calls=%async_computation.1 | async-start | bytes 655360 | tf_op jit(solution)/shard_map/all_to_all | solution.py:23
  32.4 0.2 shard_map.95
  32.7 1.9 %collective-permute-start.1 = (f32[15,80,128]{2,1,0:T(8,128)S(1)}, f32[15,80,128]{2,1,0:T(8,128)S(1)}, u32[]{:S(2)}, u32[]{:S(2)}) collective-permute-start(f32[15,80,128]{2,1,0:T(8,128)S(1)} %get-tuple-element.10), channel_id=1, source_target_pairs={{16,32},{32,16},{17,33},{33,17},{18,34},{34,18},{19,35},{35,19},{2... | collective-permute-start | bytes 1843208 | tf_op jit(solution)/shard_map/ppermute | solution.py:331
  34.6 4.3 %collective-permute-start = (f32[16,80,128]{2,1,0:T(8,128)S(1)}, f32[16,80,128]{2,1,0:T(8,128)S(1)}, u32[]{:S(2)}, u32[]{:S(2)}) collective-permute-start(f32[16,80,128]{2,1,0:T(8,128)S(1)} %get-tuple-element.9.own_ref), channel_id=1, source_target_pairs={{0,16},{16,0},{32,48},{48,32},{64,80},{80,64},{96,112},{112,96},{1... | collective-permute-start | bytes 1966088 | tf_op jit(solution)/shard_map/ppermute | solution.py:332
  38.9 3.5 %all-to-all-done.1.raw_ref = f32[16,40,128]{2,1,0:T(8,128)S(1)} async-done(((f32[16,40,128]{2,1,0:T(8,128)}), f32[16,40,128]{2,1,0:T(8,128)S(1)}, u32[]{:S(2)}, u32[]{:S(2)}) %all-to-all-start.1) | async-done | bytes 327712 | tf_op jit(solution)/shard_map/all_to_all | solution.py:23
  42.4 0.2 shard_map.96.place
  42.6 4.9 %collective-permute-done.1.far_ref = f32[15,80,128]{2,1,0:T(8,128)S(1)} collective-permute-done((f32[15,80,128]{2,1,0:T(8,128)S(1)}, f32[15,80,128]{2,1,0:T(8,128)S(1)}, u32[]{:S(2)}, u32[]{:S(2)}) %collective-permute-start.1) | collective-permute-done | bytes 614432 | tf_op jit(solution)/shard_map/ppermute | solution.py:331
  47.5 0.0 collective-permute-done.near_ref
  47.5 4.0 %shard_map.97 = f32[16,72,128]{2,1,0:T(8,128)S(1)} custom-call(f32[16,80,128]{2,1,0:T(8,128)S(1)} %get-tuple-element.9.own_ref, f32[16,80,128]{2,1,0:T(8,128)S(1)} %collective-permute-done.near_ref, f32[15,80,128]{2,1,0:T(8,128)S(1)} %collective-permute-done.1.far_ref, f32[8,72,128]{2,1,0:T(8,128)S(1)} %shard_map.96.place), custom_call_target="tpu_custom_call" | custom-call | flops 300000000 | bytes 2809856 | tf_op jit(solution)/shard_map/pallas_call | solution.py:286
  51.5 22.8 %all_to_all.15.in_ref = f32[16,72,128]{2,1,0:T(8,128)S(1)} all-to-all(f32[16,72,128]{2,1,0:T(8,128)S(1)} %shard_map.97), channel_id=1, replica_groups={{8,9,15,14,4,5,11,10,0,1,7,6,12,13,3,2},{24,25,31,30,20,21,27,26,16,17,..., dimensions={0} | all-to-all | bytes 1179648 | tf_op jit(solution)/shard_map/all_to_all | solution.py:23
  74.3 1.1 %shard_map.98 = (f32[4,8,1152]{2,1,0:T(8,128)}, f32[4,8,1152]{2,1,0:T(8,128)}, f32[4,8,1152]{2,1,0:T(8,128)}, f32[4,8,1152]{2,1,0:T(8,128)}) custom-call(f32[16,72,128]{2,1,0:T(8,128)S(1)} %all_to_all.15.in_ref), custom_call_target="tpu_custom_call" | custom-call | bytes 1179648 | tf_op jit(solution)/shard_map/pallas_call | solution.py:286
Async XLA Ops:
  2.9 24.0 %all-to-all-start = ((f32[16,80,128]{2,1,0:T(8,128)}), f32[16,80,128]{2,1,0:T(8,128)S(1)}, u32[]{:S(2)}, u32[]{:S(2)}) async-start(f32[16,80,128]{2,1,0:T(8,128)} %shard_map.93), calls=%async_computation | async-start | bytes 1310720 | tf_op jit(solution)/shard_map/all_to_all | solution.py:23
  26.9 15.5 %all-to-all-start.1 = ((f32[16,40,128]{2,1,0:T(8,128)}), f32[16,40,128]{2,1,0:T(8,128)S(1)}, u32[]{:S(2)}, u32[]{:S(2)}) async-start(f32[16,40,128]{2,1,0:T(8,128)} %shard_map.94), calls=%async_computation.1 | async-start | bytes 655360 | tf_op jit(solution)/shard_map/all_to_all | solution.py:23
  32.7 14.8 %collective-permute-start.1 = (f32[15,80,128]{2,1,0:T(8,128)S(1)}, f32[15,80,128]{2,1,0:T(8,128)S(1)}, u32[]{:S(2)}, u32[]{:S(2)}) collective-permute-start(f32[15,80,128]{2,1,0:T(8,128)S(1)} %get-tuple-element.10), channel_id=1, source_target_pairs={{16,32},{32,16},{17,33},{33,17},{18,34},{34,18},{19,35},{35,19},{2... | collective-permute-start | bytes 1843208 | tf_op jit(solution)/shard_map/ppermute | solution.py:331
  34.6 12.9 %collective-permute-start = (f32[16,80,128]{2,1,0:T(8,128)S(1)}, f32[16,80,128]{2,1,0:T(8,128)S(1)}, u32[]{:S(2)}, u32[]{:S(2)}) collective-permute-start(f32[16,80,128]{2,1,0:T(8,128)S(1)} %get-tuple-element.9.own_ref), channel_id=1, source_target_pairs={{0,16},{16,0},{32,48},{48,32},{64,80},{80,64},{96,112},{112,96},{1... | collective-permute-start | bytes 1966088 | tf_op jit(solution)/shard_map/ppermute | solution.py:332
